TPU v7x, 128 devices: a whole 4x4x4 slice. The times are simulated.
128 devices in a mesh: seq: 32 (over y, z, core), head: 4 (over x).
Axes of the slice: x: 4, y: 4, z: 4, core: 2. Of those that a mesh axis runs over, the one named last changes fastest.
Arguments:
- query_rows: bfloat16 [16384, 4096], P('seq', 'head'), may hold values from -6 to 6
- key_rows: bfloat16 [16384, 4096], P('seq', 'head'), may hold values from -6 to 6
- value_rows: bfloat16 [16384, 4096], P('seq', 'head'), may hold values from -6 to 6
- log_decay: float32 [32, 16384], P('head', 'seq'), may hold values from -1 to 0, as said below
- norm_gain: float32 [4096], P('head'), may hold values from 0.1 to 1.9
- out_weight: bfloat16 [6144, 4096], P('seq', 'head'), may hold values from -0.09375 to 0.09375
- out_grad: bfloat16 [16384, 6144], P('seq', 'head'), may hold values from -6 to 6
Outputs:
- query_grad: bfloat16 [16384, 4096], P('seq', 'head')
- key_grad: bfloat16 [16384, 4096], P('seq', 'head')
- value_grad: bfloat16 [16384, 4096], P('seq', 'head')
- weight_grad: float32 [6144, 4096], P('seq', 'head')
Inputs may be any that keep to these rules, and one draw needn't show every extreme that they name: log_decay holds the logarithm of a decay factor in (0, 1], one per head and position.
All inputs are finite; a program needn't handle non-finite values.
Results may differ from a plain program's by a relative error of at most 0.024.
Values may be sent and summed in bfloat16 or wider, within the bound.
A program may use at most 192 MiB of HBM per device.

v0:
```python
import jax
import jax.numpy as jnp
from jax import lax
from jax.experimental import pallas as pl
from jax.experimental.pallas import tpu as pltpu
from jax.sharding import PartitionSpec as P

MESH = pl.DeviceIdType.MESH
BF = jnp.bfloat16
F32 = jnp.float32
HIGH = lax.Precision.HIGHEST
EPSILON = 1e-06

ROWS = 512
HEADS = 8
WIDE = 128
COLS = 1024
UNIT = 192
HALF = 96
QUART = 48
SPAN = 768
BLK = 256
SCALE = 1.0 / 128.0

S_SIB = 0
S_X = 1
S_W = 7
S_MIX = 23
S_OD = 24
S_RS = 25
S_F1 = 41
S_F2 = 48
S_F3 = 51
S_B1 = 58
S_B2 = 65
S_B3 = 68
S_ALL = 75


def dot(a, b):
    return lax.dot_general(a, b, (((1,), (0,)), ((), ())), preferred_element_type=F32)


def dot_t0(a, b):
    return lax.dot_general(a, b, (((0,), (0,)), ((), ())), preferred_element_type=F32)


def dot_t1(a, b):
    return lax.dot_general(a, b, (((1,), (1,)), ((), ())), preferred_element_type=F32)


def kernel(
    q, k, v, ld, gain, w, g,
    dq, dk, dv, dw,
    OG, OGS, WB, ACC, XO, XI, MX, DW, R1, R2, R3, R4,
    PB, ATT, DA, CC, RN, CR,
    ST, STI, RT, RTI, EN, ENT, LL, EP,
    GS, GSI, GR, GRI, GO, GG,
    ss, rs,
):
    me = lax.axis_index("seq")
    x = lax.axis_index("head")
    y = lax.div(me, 8)
    grp = lax.rem(me, 8)
    z = lax.div(grp, 2)
    c = lax.rem(me, 2)
    o = 1 - c

    def turn(a, d):
        return lax.rem(a + d, 4)

    yn, yo, yp = turn(y, 1), turn(y, 2), turn(y, 3)
    zn, zo, zp = turn(z, 1), turn(z, 2), turn(z, 3)
    xn, xo, xp = turn(x, 1), turn(x, 2), turn(x, 3)

    def at(yy, zz, cc):
        return ((yy * 4 + zz) * 2 + cc, x)

    YN, YP, ZN, ZP = at(yn, z, c), at(yp, z, c), at(y, zn, c), at(y, zp, c)
    XN, XP = (me, xn), (me, xp)
    SIB = at(y, z, o)

    def mate(d):
        p = lax.rem(grp + d, 8)
        return p, (y * 8 + p, x)

    live = []

    def put(i, src, dst, dev):
        copy = pltpu.make_async_remote_copy(
            src_ref=src,
            dst_ref=dst,
            send_sem=ss.at[i],
            recv_sem=rs.at[i],
            device_id=dev,
            device_id_type=MESH,
        )
        copy.start()
        live.append(copy)
        return copy

    barrier = pltpu.get_barrier_semaphore()
    partners = [mate(d)[1] for d in range(1, 8)]
    partners += [at(turn(y, d), z, c) for d in (1, 2, 3)]
    partners += [XN, XP]
    for dev in partners:
        pl.semaphore_signal(barrier, inc=1, device_id=dev, device_id_type=MESH)
    pl.semaphore_wait(barrier, len(partners))

    own_rows = pl.ds(pl.multiple_of(c * ROWS, ROWS), ROWS)
    sib_rows = pl.ds(pl.multiple_of(o * ROWS, ROWS), ROWS)
    rows_a, rows_b = pl.ds(0, HALF), pl.ds(HALF, HALF)
    a_lo, a_hi = pl.ds(0, QUART), pl.ds(QUART, QUART)
    b_lo, b_hi = pl.ds(HALF, QUART), pl.ds(HALF + QUART, QUART)

    WB[y, z] = w[...]
    wa0 = put(S_W + 0, WB.at[y, z, rows_a], WB.at[y, z, rows_a], YN)
    wa1 = put(S_W + 1, WB.at[y, z, rows_a], WB.at[y, z, rows_a], YP)
    wb0 = put(S_W + 8, WB.at[y, z, rows_b], WB.at[y, z, rows_b], ZN)
    wb1 = put(S_W + 9, WB.at[y, z, rows_b], WB.at[y, z, rows_b], ZP)

    for part in range(4):
        r = pl.ds(part * 128, 128)
        rows = g[r, :]
        even = jnp.concatenate(
            [rows[:, (2 * i) * UNIT : (2 * i + 1) * UNIT] for i in range(4)], axis=1
        )
        odd = jnp.concatenate(
            [rows[:, (2 * i + 1) * UNIT : (2 * i + 2) * UNIT] for i in range(4)], axis=1
        )
        mine = jnp.where(c == 0, even, odd)
        other = jnp.where(c == 0, odd, even)
        OG[x, pl.ds(pl.multiple_of(c * ROWS + part * 128, 128), 128), :] = mine
        OGS[r, :] = other
    sib = put(S_SIB, OGS, OG.at[x, own_rows], SIB)
    xr0 = put(S_X + 0, OG.at[x, own_rows], OG.at[x, own_rows], XN)
    xl1 = put(S_X + 3, OG.at[x, own_rows], OG.at[x, own_rows], XP)

    row_i = lax.broadcasted_iota(jnp.int32, (ROWS, ROWS), 0)
    col_i = lax.broadcasted_iota(jnp.int32, (ROWS, ROWS), 1)
    upper = (row_i <= col_i).astype(F32)
    lower = (row_i >= col_i).astype(F32)
    by_rows = lax.dot_general(
        ld[...], upper, (((1,), (0,)), ((), ())), precision=HIGH, preferred_element_type=F32
    )
    by_cols = lax.dot_general(
        lower, ld[...], (((1,), (1,)), ((), ())), precision=HIGH, preferred_element_type=F32
    )
    for h in range(HEADS):
        CR[h] = by_rows[h : h + 1, :]
        CC[h] = by_cols[:, h : h + 1]

    sib.wait_recv()
    xl0 = put(S_X + 2, OG.at[x, sib_rows], OG.at[x, sib_rows], XP)
    xr1 = put(S_X + 1, OG.at[x, sib_rows], OG.at[x, sib_rows], XN)

    def head_cols(h):
        return pl.ds(pl.multiple_of(h * WIDE, WIDE), WIDE)

    def decays(h, tb, sb):
        cc = CC[h, pl.ds(tb * BLK, BLK), :]
        cr = CR[h, :, pl.ds(sb * BLK, BLK)]
        grown = jnp.exp(cc - cr)
        if tb == sb:
            t = lax.broadcasted_iota(jnp.int32, (BLK, BLK), 0)
            s = lax.broadcasted_iota(jnp.int32, (BLK, BLK), 1)
            grown = jnp.where(t >= s, grown, 0.0)
        return grown

    def blk(b):
        return pl.ds(b * BLK, BLK)

    row16 = lax.broadcasted_iota(jnp.int32, (16, WIDE), 0)

    def split3(row):
        hi = row.astype(BF).astype(F32)
        mid = (row - hi).astype(BF).astype(F32)
        lo = (row - hi - mid).astype(BF).astype(F32)
        full = jnp.where(
            row16 == 0, hi, jnp.where(row16 == 1, mid, jnp.where(row16 == 2, lo, 0.0))
        )
        return full.astype(BF)

    def join3(block):
        return jnp.sum(block.astype(F32), axis=0, keepdims=True)

    def forward_head(h, _):
        hs = head_cols(h)
        for tb in range(2):
            out = jnp.zeros((BLK, WIDE), F32)
            for sb in range(tb + 1):
                scores = dot_t1(q[blk(tb), hs], k[blk(sb), hs])
                p = (scores * decays(h, tb, sb)).astype(BF)
                PB[h, blk(tb), blk(sb)] = p
                out = out + dot(p, v[blk(sb), hs])
            ATT[blk(tb), hs] = out
        total = CR[h, :, pl.ds(ROWS - WIDE, WIDE)][:, WIDE - 1 : WIDE]
        kd = (k[:, hs].astype(F32) * jnp.exp(total - CC[h])).astype(BF)
        ST[h, pl.ds(0, WIDE), :] = dot_t0(kd, v[:, hs]).astype(BF)
        ST[h, pl.ds(WIDE, 16), :] = split3(jnp.broadcast_to(total, (1, WIDE)))
        return 0

    lax.fori_loop(0, 4, forward_head, 0)

    wa0.wait_recv()
    wa2 = put(S_W + 2, WB.at[yp, z, a_lo], WB.at[yp, z, a_lo], YN)
    wa1.wait_recv()
    wa3 = put(S_W + 3, WB.at[yn, z, a_hi], WB.at[yn, z, a_hi], YP)
    wb0.wait_recv()
    wb2 = put(S_W + 10, WB.at[y, zp, b_lo], WB.at[y, zp, b_lo], ZN)
    wb1.wait_recv()
    wb3 = put(S_W + 11, WB.at[y, zn, b_hi], WB.at[y, zn, b_hi], ZP)

    lax.fori_loop(4, 8, forward_head, 0)

    STI[grp] = ST[grp]
    f1 = []
    for d in range(1, 8):
        p, dev = mate(d)
        f1.append(put(S_F1 + d - 1, ST.at[p], STI.at[grp], dev))

    wa2.wait_recv()
    wa3.wait_recv()
    wa4 = put(S_W + 4, WB.at[:, z, rows_a], WB.at[:, z, rows_a], ZN)
    wa5 = put(S_W + 5, WB.at[:, z, rows_a], WB.at[:, z, rows_a], ZP)
    wb2.wait_recv()
    wb3.wait_recv()
    wb4 = put(S_W + 12, WB.at[y, :, rows_b], WB.at[y, :, rows_b], YN)
    wb5 = put(S_W + 13, WB.at[y, :, rows_b], WB.at[y, :, rows_b], YP)

    for copy in f1:
        copy.wait_recv()

    def chain(i, carry):
        state, logs = carry
        log_i = join3(STI[i, pl.ds(WIDE, 16), :])
        LL[i] = state
        EP[i] = logs
        state = jnp.exp(log_i) * state + STI[i, pl.ds(0, WIDE), :].astype(F32)
        return state, logs + log_i

    row_state, row_logs = lax.fori_loop(
        0, 8, chain, (jnp.zeros((WIDE, WIDE), F32), jnp.zeros((1, WIDE), F32))
    )
    RT[pl.ds(0, WIDE), :] = row_state.astype(BF)
    RT[pl.ds(WIDE, 16), :] = split3(row_logs)
    RTI[y] = RT[...]
    f2 = [
        put(S_F2 + d - 1, RT, RTI.at[y], at(turn(y, d), z, c)) for d in (1, 2, 3)
    ]
    for copy in f2:
        copy.wait_recv()
    carried = jnp.zeros((WIDE, WIDE), F32)
    for yy in range(3):
        grown = jnp.exp(join3(RTI[yy, pl.ds(WIDE, 16), :])) * carried
        grown = grown + RTI[yy, pl.ds(0, WIDE), :].astype(F32)
        carried = jnp.where(yy < y, grown, carried)

    def enter(i, _):
        EN[i] = (LL[i] + jnp.exp(EP[i]) * carried).astype(BF)
        return 0

    lax.fori_loop(0, 8, enter, 0)
    ENT[grp] = EN[grp]
    f3 = []
    for d in range(1, 8):
        p, dev = mate(d)
        f3.append(put(S_F3 + d - 1, EN.at[p], ENT.at[grp], dev))
    for copy in f3:
        copy.wait_recv()

    def attend_head(h, _):
        hs = head_cols(h)
        att = ATT[:, hs] + jnp.exp(CC[h]) * dot(q[:, hs], ENT[h])
        r = lax.rsqrt(jnp.mean(att * att, axis=-1, keepdims=True) + EPSILON)
        scaled = att * r
        ATT[:, hs] = scaled
        RN[h] = r
        MX[c, :, hs] = (scaled * gain[:, hs]).astype(BF)
        return 0

    lax.fori_loop(0, HEADS, attend_head, 0)
    mix = put(S_MIX, MX.at[c], MX.at[c], SIB)

    wa4.wait_recv()
    wa6 = put(S_W + 6, WB.at[:, zp, a_lo], WB.at[:, zp, a_lo], ZN)
    wa5.wait_recv()
    wa7 = put(S_W + 7, WB.at[:, zn, a_hi], WB.at[:, zn, a_hi], ZP)
    wb4.wait_recv()
    wb6 = put(S_W + 14, WB.at[yp, :, b_lo], WB.at[yp, :, b_lo], YN)
    wb5.wait_recv()
    wb7 = put(S_W + 15, WB.at[yn, :, b_hi], WB.at[yn, :, b_hi], YP)

    def weight_term(xx):
        def tile(i, _):
            pair = lax.div(i, 2)
            n = lax.rem(i, 2)
            ms = pl.ds(pl.multiple_of(pair * 384, 384), 384)
            ns = pl.ds(pl.multiple_of(n * 512, 512), 512)
            term = dot_t0(OG[xx, pl.ds(0, ROWS), ms], MX[0, :, ns])
            term = term + dot_t0(OG[xx, pl.ds(ROWS, ROWS), ms], MX[1, :, ns])
            DW[xx, pl.ds(2 * pair, 2), :, ns] = term.reshape(2, UNIT, 512).astype(BF)
            return 0

        lax.fori_loop(0, 4, tile, 0)

    def delta_term(xx, first, half):
        def tile(i, _):
            m = lax.div(i, 2)
            n = lax.rem(i, 2)
            ms = pl.ds(pl.multiple_of(half * ROWS + m * BLK, BLK), BLK)
            ns = pl.ds(pl.multiple_of(n * 512, 512), 512)
            term = dot(OG[xx, ms, :], WB[xx, :, :, ns].reshape(SPAN, 512))
            if first:
                ACC[ms, ns] = term
            else:
                ACC[ms, ns] += term
            return 0

        lax.fori_loop(0, 4, tile, 0)

    mix.wait_recv()
    weight_term(x)

    xr0.wait_recv()
    xr2 = put(S_X + 4, OG.at[xp, own_rows], OG.at[xp, own_rows], XN)
    xl0.wait_recv()
    xl2 = put(S_X + 5, OG.at[xn, sib_rows], OG.at[xn, sib_rows], XP)

    for copy in (wa6, wa7, wb6, wb7):
        copy.wait_recv()
    delta_term(x, True, o)
    delta_term(x, True, c)
    xr1.wait_recv()
    xl1.wait_recv()
    for xx in (xp, xn):
        weight_term(xx)
        delta_term(xx, False, o)
        delta_term(xx, False, c)
    xr2.wait_recv()
    xl2.wait_recv()
    weight_term(xo)

    ra0 = put(S_RS + 0, DW.at[:, zo, a_lo], R1.at[0, 0], ZN)
    ra1 = put(S_RS + 1, DW.at[:, zo, a_hi], R1.at[0, 1], ZP)
    rb0 = put(S_RS + 8, DW.at[yo, :, b_lo], R1.at[1, 0], YN)
    rb1 = put(S_RS + 9, DW.at[yo, :, b_hi], R1.at[1, 1], YP)

    delta_term(xo, False, o)
    XO[...] = ACC[sib_rows, :].astype(BF)
    od = put(S_OD, XO, XI, SIB)
    delta_term(xo, False, c)
    od.wait_recv()

    def norm_back_head(h, _):
        hs = head_cols(h)
        delta = ACC[own_rows, hs] + XI[:, hs].astype(F32)
        scaled = ATT[:, hs]
        gg = delta * gain[:, hs]
        da = RN[h] * (gg - scaled * jnp.mean(gg * scaled, axis=-1, keepdims=True))
        da = da.astype(BF)
        DA[:, hs] = da
        qd = (q[:, hs].astype(F32) * jnp.exp(CC[h])).astype(BF)
        GS[h] = dot_t0(qd, da).astype(BF)
        return 0

    lax.fori_loop(0, HEADS, norm_back_head, 0)

    GSI[grp] = GS[grp]
    b1 = []
    for d in range(1, 8):
        p, dev = mate(d)
        b1.append(put(S_B1 + d - 1, GS.at[p], GSI.at[grp], dev))

    def add_to(target, more):
        return (target.astype(F32) + more.astype(F32)).astype(BF)

    ra0.wait_recv()
    for i in range(4):
        DW[i, zn, a_lo] = add_to(DW[i, zn, a_lo], R1[0, 0, i])
    ra2 = put(S_RS + 2, DW.at[:, zn, rows_a], R2.at[0, 0], ZN)
    ra1.wait_recv()
    for i in range(4):
        DW[i, zp, a_hi] = add_to(DW[i, zp, a_hi], R1[0, 1, i])
    ra3 = put(S_RS + 3, DW.at[:, zp, rows_a], R2.at[0, 1], ZP)
    rb0.wait_recv()
    for i in range(4):
        DW[yn, i, b_lo] = add_to(DW[yn, i, b_lo], R1[1, 0, i])
    rb2 = put(S_RS + 10, DW.at[yn, :, rows_b], R2.at[1, 0], YN)
    rb1.wait_recv()
    for i in range(4):
        DW[yp, i, b_hi] = add_to(DW[yp, i, b_hi], R1[1, 1, i])
    rb3 = put(S_RS + 11, DW.at[yp, :, rows_b], R2.at[1, 1], YP)

    for copy in b1:
        copy.wait_recv()

    def chain_back(n, carry):
        i = 7 - n
        state, logs = carry
        log_i = join3(STI[i, pl.ds(WIDE, 16), :])
        LL[i] = state
        EP[i] = logs
        state = jnp.exp(log_i) * state + GSI[i].astype(F32)
        return state, logs + log_i

    row_back, _ = lax.fori_loop(
        0, 8, chain_back, (jnp.zeros((WIDE, WIDE), F32), jnp.zeros((1, WIDE), F32))
    )
    GR[...] = row_back.astype(BF)
    GRI[y] = GR[...]
    b2 = [
        put(S_B2 + d - 1, GR, GRI.at[y], at(turn(y, d), z, c)) for d in (1, 2, 3)
    ]

    def local_back_head(h, _):
        hs = head_cols(h)
        dk_blk = [None, None]
        dv_blk = [None, None]
        for tb in range(2):
            da = DA[blk(tb), hs]
            out = jnp.exp(CC[h, blk(tb), :]) * dot_t1(da, ENT[h])
            for sb in range(tb + 1):
                dp = (dot_t1(da, v[blk(sb), hs]) * decays(h, tb, sb)).astype(BF)
                out = out + dot(dp, k[blk(sb), hs])
                k_term = dot_t0(dp, q[blk(tb), hs])
                v_term = dot_t0(PB[h, blk(tb), blk(sb)], da)
                dk_blk[sb] = k_term if dk_blk[sb] is None else dk_blk[sb] + k_term
                dv_blk[sb] = v_term if dv_blk[sb] is None else dv_blk[sb] + v_term
            dq[blk(tb), hs] = out.astype(BF)
        for sb in range(2):
            ACC[blk(sb), hs] = dk_blk[sb]
            ACC[blk(2 + sb), hs] = dv_blk[sb]
        return 0

    lax.fori_loop(0, 4, local_back_head, 0)

    for copy in b2:
        copy.wait_recv()
    carried_back = jnp.zeros((WIDE, WIDE), F32)
    for yy in (3, 2, 1):
        grown = jnp.exp(join3(RTI[yy, pl.ds(WIDE, 16), :])) * carried_back
        grown = grown + GRI[yy].astype(F32)
        carried_back = jnp.where(yy > y, grown, carried_back)

    def leave(i, _):
        GO[i] = (LL[i] + jnp.exp(EP[i]) * carried_back).astype(BF)
        return 0

    lax.fori_loop(0, 8, leave, 0)
    GG[grp] = GO[grp]
    b3 = []
    for d in range(1, 8):
        p, dev = mate(d)
        b3.append(put(S_B3 + d - 1, GO.at[p], GG.at[grp], dev))

    lax.fori_loop(4, 8, local_back_head, 0)

    ra2.wait_recv()
    ra3.wait_recv()
    for i in range(4):
        DW[i, z, rows_a] = (
            DW[i, z, rows_a].astype(F32) + R2[0, 0, i].astype(F32) + R2[0, 1, i].astype(F32)
        ).astype(BF)
    ra4 = put(S_RS + 4, DW.at[yo, z, a_lo], R3.at[0, 0], YN)
    ra5 = put(S_RS + 5, DW.at[yo, z, a_hi], R3.at[0, 1], YP)
    rb2.wait_recv()
    rb3.wait_recv()
    for i in range(4):
        DW[y, i, rows_b] = (
            DW[y, i, rows_b].astype(F32) + R2[1, 0, i].astype(F32) + R2[1, 1, i].astype(F32)
        ).astype(BF)
    rb4 = put(S_RS + 12, DW.at[y, zo, b_lo], R3.at[1, 0], ZN)
    rb5 = put(S_RS + 13, DW.at[y, zo, b_hi], R3.at[1, 1], ZP)

    for copy in b3:
        copy.wait_recv()

    def last_head(h, _):
        hs = head_cols(h)
        total = CR[h, :, pl.ds(ROWS - WIDE, WIDE)][:, WIDE - 1 : WIDE]
        tail = jnp.exp(total - CC[h])
        dk[:, hs] = (ACC[pl.ds(0, ROWS), hs] + tail * dot_t1(v[:, hs], GG[h])).astype(BF)
        dv[:, hs] = (ACC[pl.ds(ROWS, ROWS), hs] + tail * dot(k[:, hs], GG[h])).astype(BF)
        return 0

    lax.fori_loop(0, 4, last_head, 0)

    ra4.wait_recv()
    DW[yn, z, a_lo] = add_to(DW[yn, z, a_lo], R3[0, 0])
    ra6 = put(S_RS + 6, DW.at[yn, z, rows_a], R4.at[0, 0], YN)
    ra5.wait_recv()
    DW[yp, z, a_hi] = add_to(DW[yp, z, a_hi], R3[0, 1])
    ra7 = put(S_RS + 7, DW.at[yp, z, rows_a], R4.at[0, 1], YP)
    rb4.wait_recv()
    DW[y, zn, b_lo] = add_to(DW[y, zn, b_lo], R3[1, 0])
    rb6 = put(S_RS + 14, DW.at[y, zn, rows_b], R4.at[1, 0], ZN)
    rb5.wait_recv()
    DW[y, zp, b_hi] = add_to(DW[y, zp, b_hi], R3[1, 1])
    rb7 = put(S_RS + 15, DW.at[y, zp, rows_b], R4.at[1, 1], ZP)

    lax.fori_loop(4, 8, last_head, 0)

    ra6.wait_recv()
    ra7.wait_recv()
    dw[rows_a, :] = (
        DW[y, z, rows_a].astype(F32) + R4[0, 0].astype(F32) + R4[0, 1].astype(F32)
    ) * SCALE
    rb6.wait_recv()
    rb7.wait_recv()
    dw[rows_b, :] = (
        DW[y, z, rows_b].astype(F32) + R4[1, 0].astype(F32) + R4[1, 1].astype(F32)
    ) * SCALE

    for copy in live:
        copy.wait_send()


def body(query_rows, key_rows, value_rows, log_decay, norm_gain, out_weight, out_grad):
    vm = pltpu.VMEM
    scratch = [
        vm((4, 2 * ROWS, SPAN), BF),
        vm((ROWS, SPAN), BF),
        vm((4, 4, UNIT, COLS), BF),
        vm((2 * ROWS, COLS), F32),
        vm((ROWS, COLS), BF),
        vm((ROWS, COLS), BF),
        vm((2, ROWS, COLS), BF),
        vm((4, 4, UNIT, COLS), BF),
        vm((2, 2, 4, QUART, COLS), BF),
        vm((2, 2, 4, HALF, COLS), BF),
        vm((2, 2, QUART, COLS), BF),
        vm((2, 2, HALF, COLS), BF),
        vm((HEADS, ROWS, ROWS), BF),
        vm((ROWS, COLS), F32),
        vm((ROWS, COLS), BF),
        vm((HEADS, ROWS, 1), F32),
        vm((HEADS, ROWS, 1), F32),
        vm((HEADS, 1, ROWS), F32),
        vm((8, WIDE + 16, WIDE), BF),
        vm((8, WIDE + 16, WIDE), BF),
        vm((WIDE + 16, WIDE), BF),
        vm((4, WIDE + 16, WIDE), BF),
        vm((8, WIDE, WIDE), BF),
        vm((8, WIDE, WIDE), BF),
        vm((8, WIDE, WIDE), F32),
        vm((8, 1, WIDE), F32),
        vm((8, WIDE, WIDE), BF),
        vm((8, WIDE, WIDE), BF),
        vm((WIDE, WIDE), BF),
        vm((4, WIDE, WIDE), BF),
        vm((8, WIDE, WIDE), BF),
        vm((8, WIDE, WIDE), BF),
        pltpu.SemaphoreType.DMA((S_ALL,)),
        pltpu.SemaphoreType.DMA((S_ALL,)),
    ]
    spec = pl.BlockSpec(memory_space=pltpu.VMEM)
    return pl.pallas_call(
        kernel,
        out_shape=(
            jax.ShapeDtypeStruct((ROWS, COLS), BF),
            jax.ShapeDtypeStruct((ROWS, COLS), BF),
            jax.ShapeDtypeStruct((ROWS, COLS), BF),
            jax.ShapeDtypeStruct((UNIT, COLS), F32),
        ),
        in_specs=[spec] * 7,
        out_specs=(spec,) * 4,
        scratch_shapes=scratch,
        compiler_params=pltpu.CompilerParams(
            collective_id=0, has_side_effects=True, vmem_limit_bytes=62 * 2**20
        ),
    )(
        query_rows,
        key_rows,
        value_rows,
        log_decay,
        norm_gain.reshape(1, COLS),
        out_weight,
        out_grad,
    )


def solution(mesh):
    both = P("seq", "head")
    return jax.shard_map(
        body,
        mesh=mesh,
        in_specs=(both, both, both, P("head", "seq"), P("head"), both, both),
        out_specs=(both, both, both, both),
        check_vma=False,
    )
```

profile of v0, /device:TPU:4, one launch (start us, length us, event | category | flops | bytes accessed | tf_op | source)
XLA Modules:
  0.0 128.3 jit_solution(5171916705336305423)
XLA Ops:
  0.6 122.4 %shard_map.102 = (bf16[512,1024]{1,0:T(8,128)(2,1)}, bf16[512,1024]{1,0:T(8,128)(2,1)}, bf16[512,1024]{1,0:T(8,128)(2,1)}, f32[192,1024]{1,0:T(8,128)}) custom-call(bf16[512,1024]{1,0:T(8,128)(2,1)} %q.1, bf16[512,1024]{1,0:T(8,128)(2,1)} %k.1, bf16[512,1024]{1,0:T(8,128)(2,1)} %v.1, f32[8,512]{1,0:T(8,128)} %ld.1, f32[1,1024]{1,0:T(1,128)} %bitcast.1, ...), custom_call_target="tpu_custom_call" | custom-call | tf_op jit(solution)/shard_map/pallas_call | solution.py:558
  123.0 0.0 copy-start.1
  123.0 0.0 copy-start
  123.0 2.4 %copy.15 = bf16[512,1024]{1,0:T(8,128)(2,1)} copy(bf16[512,1024]{1,0:T(8,128)(2,1)} %get-tuple-element.8) | data formatting | bytes 2097152
  125.4 0.0 copy-done.1
  125.4 0.0 copy-start.2
  125.4 1.0 copy.16
  126.4 0.0 copy-done
  126.4 1.0 copy.17
  127.4 0.0 copy-done.2
  127.4 0.9 copy.18
Async XLA Ops:
  123.0 2.4 %copy-start.1 = (bf16[512,1024]{1,0:T(8,128)(2,1)S(1)}, bf16[512,1024]{1,0:T(8,128)(2,1)}, u32[]{:S(2)}) copy-start(bf16[512,1024]{1,0:T(8,128)(2,1)} %get-tuple-element.9) | copy-start | bytes 3145732
  123.0 3.4 %copy-start = (bf16[512,1024]{1,0:T(8,128)(2,1)S(1)}, bf16[512,1024]{1,0:T(8,128)(2,1)}, u32[]{:S(2)}) copy-start(bf16[512,1024]{1,0:T(8,128)(2,1)} %get-tuple-element.10) | copy-start | bytes 3145732
  125.4 1.9 %copy-start.2 = (f32[192,1024]{1,0:T(8,128)S(1)}, f32[192,1024]{1,0:T(8,128)}, u32[]{:S(2)}) copy-start(f32[192,1024]{1,0:T(8,128)} %get-tuple-element.11) | copy-start | bytes 2359300
where the time goes:
time: 130 us; the launch traced here: 128 us
  Pallas kernels  122 us (94%)
  local copies, waits for them, and re-layouts  5.24 us (4%)
    pallas_call x1, Pallas kernels, body(): pl.pallas_call(kernel, out_shape=(jax.ShapeDtypeStruct((ROWS, COLS), BF),...  122 us
    unnamed x10, local copies, waits for them, and re-layouts  5.24 us

commit v1 on v0

--- a/solution.py
+++ b/solution.py
@@ -24,17 +24,19 @@
 
 S_SIB = 0
 S_X = 1
-S_W = 7
-S_MIX = 23
-S_OD = 24
-S_RS = 25
-S_F1 = 41
-S_F2 = 48
-S_F3 = 51
-S_B1 = 58
-S_B2 = 65
-S_B3 = 68
-S_ALL = 75
+S_MIX = 7
+S_OD = 8
+S_W = 10
+S_A1 = 42
+S_A2 = 50
+S_RS = 58
+S_F1 = 70
+S_F2 = 77
+S_F3 = 80
+S_B1 = 87
+S_B2 = 94
+S_B3 = 97
+S_ALL = 104
 
 
 def dot(a, b):
@@ -52,7 +54,7 @@
 def kernel(
     q, k, v, ld, gain, w, g,
     dq, dk, dv, dw,
-    OG, OGS, WB, ACC, XO, XI, MX, DW, R1, R2, R3, R4,
+    OG, OGS, WB, ACC, XO, XI, MX, DW, R1, R2, R3, R4, R1B, R2B,
     PB, ATT, DA, CC, RN, CR,
     ST, STI, RT, RTI, EN, ENT, LL, EP,
     GS, GSI, GR, GRI, GO, GG,
@@ -86,8 +88,8 @@
 
     live = []
 
-    def put(i, src, dst, dev):
-        copy = pltpu.make_async_remote_copy(
+    def make(i, src, dst, dev):
+        return pltpu.make_async_remote_copy(
             src_ref=src,
             dst_ref=dst,
             send_sem=ss.at[i],
@@ -95,9 +97,15 @@
             device_id=dev,
             device_id_type=MESH,
         )
+
+    def put(i, src, dst, dev):
+        copy = make(i, src, dst, dev)
         copy.start()
         live.append(copy)
         return copy
+
+    def same(i, ref, dev):
+        return put(i, ref, ref, dev)
 
     barrier = pltpu.get_barrier_semaphore()
     partners = [mate(d)[1] for d in range(1, 8)]
@@ -109,15 +117,12 @@
 
     own_rows = pl.ds(pl.multiple_of(c * ROWS, ROWS), ROWS)
     sib_rows = pl.ds(pl.multiple_of(o * ROWS, ROWS), ROWS)
-    rows_a, rows_b = pl.ds(0, HALF), pl.ds(HALF, HALF)
-    a_lo, a_hi = pl.ds(0, QUART), pl.ds(QUART, QUART)
-    b_lo, b_hi = pl.ds(HALF, QUART), pl.ds(HALF + QUART, QUART)
-
-    WB[y, z] = w[...]
-    wa0 = put(S_W + 0, WB.at[y, z, rows_a], WB.at[y, z, rows_a], YN)
-    wa1 = put(S_W + 1, WB.at[y, z, rows_a], WB.at[y, z, rows_a], YP)
-    wb0 = put(S_W + 8, WB.at[y, z, rows_b], WB.at[y, z, rows_b], ZN)
-    wb1 = put(S_W + 9, WB.at[y, z, rows_b], WB.at[y, z, rows_b], ZP)
+
+    WB[y, z] = w[...].reshape(2, 2, QUART, COLS)
+    wy0 = same(S_W + 0, WB.at[y, z], YN)
+    wy1 = same(S_W + 1, WB.at[y, z], YP)
+    wz0 = same(S_W + 2, WB.at[y, z], ZN)
+    wz1 = same(S_W + 3, WB.at[y, z], ZP)
 
     for part in range(4):
         r = pl.ds(part * 128, 128)
@@ -184,7 +189,7 @@
     def join3(block):
         return jnp.sum(block.astype(F32), axis=0, keepdims=True)
 
-    def forward_head(h, _):
+    def forward_head(h):
         hs = head_cols(h)
         for tb in range(2):
             out = jnp.zeros((BLK, WIDE), F32)
@@ -198,35 +203,38 @@
         kd = (k[:, hs].astype(F32) * jnp.exp(total - CC[h])).astype(BF)
         ST[h, pl.ds(0, WIDE), :] = dot_t0(kd, v[:, hs]).astype(BF)
         ST[h, pl.ds(WIDE, 16), :] = split3(jnp.broadcast_to(total, (1, WIDE)))
+
+    def first(d):
+        p, dev = mate(d)
+        return make(S_F1 + d - 1, ST.at[p], STI.at[grp], dev)
+
+    def forward_step(d, _):
+        forward_head(lax.rem(grp + d, 8))
+        first(d).start()
         return 0
 
-    lax.fori_loop(0, 4, forward_head, 0)
-
-    wa0.wait_recv()
-    wa2 = put(S_W + 2, WB.at[yp, z, a_lo], WB.at[yp, z, a_lo], YN)
-    wa1.wait_recv()
-    wa3 = put(S_W + 3, WB.at[yn, z, a_hi], WB.at[yn, z, a_hi], YP)
-    wb0.wait_recv()
-    wb2 = put(S_W + 10, WB.at[y, zp, b_lo], WB.at[y, zp, b_lo], ZN)
-    wb1.wait_recv()
-    wb3 = put(S_W + 11, WB.at[y, zn, b_hi], WB.at[y, zn, b_hi], ZP)
-
-    lax.fori_loop(4, 8, forward_head, 0)
-
+    lax.fori_loop(1, 8, forward_step, 0)
+    forward_head(grp)
     STI[grp] = ST[grp]
-    f1 = []
-    for d in range(1, 8):
-        p, dev = mate(d)
-        f1.append(put(S_F1 + d - 1, ST.at[p], STI.at[grp], dev))
-
-    wa2.wait_recv()
-    wa3.wait_recv()
-    wa4 = put(S_W + 4, WB.at[:, z, rows_a], WB.at[:, z, rows_a], ZN)
-    wa5 = put(S_W + 5, WB.at[:, z, rows_a], WB.at[:, z, rows_a], ZP)
-    wb2.wait_recv()
-    wb3.wait_recv()
-    wb4 = put(S_W + 12, WB.at[y, :, rows_b], WB.at[y, :, rows_b], YN)
-    wb5 = put(S_W + 13, WB.at[y, :, rows_b], WB.at[y, :, rows_b], YP)
+    f1 = [first(d) for d in range(1, 8)]
+    live += f1
+
+    wy0.wait_recv()
+    wyf0 = same(S_W + 4, WB.at[yp, z, :, 0], YN)
+    wyp0 = same(S_W + 5, WB.at[yp, z, 0], ZN)
+    wyp1 = same(S_W + 6, WB.at[yp, z, 0], ZP)
+    wy1.wait_recv()
+    wyf1 = same(S_W + 7, WB.at[yn, z, :, 1], YP)
+    wyn0 = same(S_W + 8, WB.at[yn, z, 0], ZN)
+    wyn1 = same(S_W + 9, WB.at[yn, z, 0], ZP)
+    wz0.wait_recv()
+    wzf0 = same(S_W + 10, WB.at[y, zp, :, 0], ZN)
+    wzp0 = same(S_W + 11, WB.at[y, zp, 1], YN)
+    wzp1 = same(S_W + 12, WB.at[y, zp, 1], YP)
+    wz1.wait_recv()
+    wzf1 = same(S_W + 13, WB.at[y, zn, :, 1], ZP)
+    wzn0 = same(S_W + 14, WB.at[y, zn, 1], YN)
+    wzn1 = same(S_W + 15, WB.at[y, zn, 1], YP)
 
     for copy in f1:
         copy.wait_recv()
@@ -266,6 +274,31 @@
     for d in range(1, 8):
         p, dev = mate(d)
         f3.append(put(S_F3 + d - 1, EN.at[p], ENT.at[grp], dev))
+
+    wyf0.wait_recv()
+    wyf1.wait_recv()
+    wyo0 = same(S_W + 16, WB.at[yo, z, 0], ZN)
+    wyo1 = same(S_W + 17, WB.at[yo, z, 0], ZP)
+    wzf0.wait_recv()
+    wzf1.wait_recv()
+    wzo0 = same(S_W + 18, WB.at[y, zo, 1], YN)
+    wzo1 = same(S_W + 19, WB.at[y, zo, 1], YP)
+    w3 = []
+    for i, (copy, ref, dev) in enumerate(
+        (
+            (wyp0, WB.at[yp, zp, 0, 0], ZN),
+            (wyp1, WB.at[yp, zn, 0, 1], ZP),
+            (wzp0, WB.at[yp, zp, 1, 0], YN),
+            (wzp1, WB.at[yn, zp, 1, 1], YP),
+            (wyn0, WB.at[yn, zp, 0, 0], ZN),
+            (wyn1, WB.at[yn, zn, 0, 1], ZP),
+            (wzn0, WB.at[yp, zn, 1, 0], YN),
+            (wzn1, WB.at[yn, zn, 1, 1], YP),
+        )
+    ):
+        copy.wait_recv()
+        w3.append(same(S_W + 20 + i, ref, dev))
+
     for copy in f3:
         copy.wait_recv()
 
@@ -282,14 +315,16 @@
     lax.fori_loop(0, HEADS, attend_head, 0)
     mix = put(S_MIX, MX.at[c], MX.at[c], SIB)
 
-    wa4.wait_recv()
-    wa6 = put(S_W + 6, WB.at[:, zp, a_lo], WB.at[:, zp, a_lo], ZN)
-    wa5.wait_recv()
-    wa7 = put(S_W + 7, WB.at[:, zn, a_hi], WB.at[:, zn, a_hi], ZP)
-    wb4.wait_recv()
-    wb6 = put(S_W + 14, WB.at[yp, :, b_lo], WB.at[yp, :, b_lo], YN)
-    wb5.wait_recv()
-    wb7 = put(S_W + 15, WB.at[yn, :, b_hi], WB.at[yn, :, b_hi], YP)
+    for i, (copy, ref, dev) in enumerate(
+        (
+            (wyo0, WB.at[yo, zp, 0, 0], ZN),
+            (wyo1, WB.at[yo, zn, 0, 1], ZP),
+            (wzo0, WB.at[yp, zo, 1, 0], YN),
+            (wzo1, WB.at[yn, zo, 1, 1], YP),
+        )
+    ):
+        copy.wait_recv()
+        w3.append(same(S_W + 28 + i, ref, dev))
 
     def weight_term(xx):
         def tile(i, _):
@@ -299,7 +334,9 @@
             ns = pl.ds(pl.multiple_of(n * 512, 512), 512)
             term = dot_t0(OG[xx, pl.ds(0, ROWS), ms], MX[0, :, ns])
             term = term + dot_t0(OG[xx, pl.ds(ROWS, ROWS), ms], MX[1, :, ns])
-            DW[xx, pl.ds(2 * pair, 2), :, ns] = term.reshape(2, UNIT, 512).astype(BF)
+            DW[xx, pl.ds(2 * pair, 2), :, :, :, ns] = (
+                term.astype(BF).reshape(2, 2, 2, QUART, 512)
+            )
             return 0
 
         lax.fori_loop(0, 4, tile, 0)
@@ -310,7 +347,7 @@
             n = lax.rem(i, 2)
             ms = pl.ds(pl.multiple_of(half * ROWS + m * BLK, BLK), BLK)
             ns = pl.ds(pl.multiple_of(n * 512, 512), 512)
-            term = dot(OG[xx, ms, :], WB[xx, :, :, ns].reshape(SPAN, 512))
+            term = dot(OG[xx, ms, :], WB[xx, :, :, :, :, ns].reshape(SPAN, 512))
             if first:
                 ACC[ms, ns] = term
             else:
@@ -319,40 +356,155 @@
 
         lax.fori_loop(0, 4, tile, 0)
 
+    def add_to(target, *more):
+        total = target.astype(F32)
+        for term in more:
+            total = total + term.astype(F32)
+        return total.astype(BF)
+
+    b1lo = make(S_RS + 0, DW.at[yo, :, 1, 0], R1B.at[0], YN)
+    b1hi = make(S_RS + 1, DW.at[yo, :, 1, 1], R1B.at[1], YP)
+    b2n = make(S_RS + 2, DW.at[yn, :, 1], R2B.at[0], YN)
+    b2p = make(S_RS + 3, DW.at[yp, :, 1], R2B.at[1], YP)
+    c1lo = make(S_RS + 4, DW.at[yo, z, 0, 0], R3.at[0, 0], YN)
+    c1hi = make(S_RS + 5, DW.at[yo, z, 0, 1], R3.at[0, 1], YP)
+    c2n = make(S_RS + 6, DW.at[yn, z, 0], R4.at[0, 0], YN)
+    c2p = make(S_RS + 7, DW.at[yp, z, 0], R4.at[0, 1], YP)
+    d1lo = make(S_RS + 8, DW.at[y, zo, 1, 0], R3.at[1, 0], ZN)
+    d1hi = make(S_RS + 9, DW.at[y, zo, 1, 1], R3.at[1, 1], ZP)
+    d2n = make(S_RS + 10, DW.at[y, zn, 1], R4.at[1, 0], ZN)
+    d2p = make(S_RS + 11, DW.at[y, zp, 1], R4.at[1, 1], ZP)
+    live += [b1lo, b1hi, b2n, b2p, c1lo, c1hi, c2n, c2p, d1lo, d1hi, d2n, d2p]
+    a1 = {}
+    a2 = {}
+
+    def reduce_1(j, xx):
+        a1[j] = (
+            put(S_A1 + 2 * j, DW.at[xx, zo, 0, 0], R1.at[0, j], ZN),
+            put(S_A1 + 2 * j + 1, DW.at[xx, zo, 0, 1], R1.at[1, j], ZP),
+        )
+
+        @pl.when(xx == yo)
+        def _():
+            b1lo.start()
+            b1hi.start()
+
+    def reduce_2(j, xx):
+        a1[j][0].wait_recv()
+        DW[xx, zn, 0, 0] = add_to(DW[xx, zn, 0, 0], R1[0, j])
+        to_n = put(S_A2 + 2 * j, DW.at[xx, zn, 0], R2.at[0, j], ZN)
+        a1[j][1].wait_recv()
+        DW[xx, zp, 0, 1] = add_to(DW[xx, zp, 0, 1], R1[1, j])
+        to_p = put(S_A2 + 2 * j + 1, DW.at[xx, zp, 0], R2.at[1, j], ZP)
+        a2[j] = (to_n, to_p)
+
+        @pl.when(xx == yn)
+        def _():
+            b1lo.wait_recv()
+            for i in range(4):
+                DW[yn, i, 1, 0] = add_to(DW[yn, i, 1, 0], R1B[0, i])
+            b2n.start()
+
+        @pl.when(xx == yp)
+        def _():
+            b1hi.wait_recv()
+            for i in range(4):
+                DW[yp, i, 1, 1] = add_to(DW[yp, i, 1, 1], R1B[1, i])
+            b2p.start()
+
+    def reduce_3(j, xx):
+        a2[j][0].wait_recv()
+        a2[j][1].wait_recv()
+        DW[xx, z, 0] = add_to(DW[xx, z, 0], R2[0, j], R2[1, j])
+
+        @pl.when(xx == yo)
+        def _():
+            c1lo.start()
+            c1hi.start()
+
+        @pl.when(xx == y)
+        def _():
+            b2n.wait_recv()
+            b2p.wait_recv()
+            for i in range(4):
+                DW[y, i, 1] = add_to(DW[y, i, 1], R2B[0, i], R2B[1, i])
+            d1lo.start()
+            d1hi.start()
+
+    def reduce_4(j, xx):
+        @pl.when(xx == yn)
+        def _():
+            c1lo.wait_recv()
+            DW[yn, z, 0, 0] = add_to(DW[yn, z, 0, 0], R3[0, 0])
+            c2n.start()
+
+        @pl.when(xx == yp)
+        def _():
+            c1hi.wait_recv()
+            DW[yp, z, 0, 1] = add_to(DW[yp, z, 0, 1], R3[0, 1])
+            c2p.start()
+
+        @pl.when(xx == y)
+        def _():
+            d1lo.wait_recv()
+            DW[y, zn, 1, 0] = add_to(DW[y, zn, 1, 0], R3[1, 0])
+            d2n.start()
+            d1hi.wait_recv()
+            DW[y, zp, 1, 1] = add_to(DW[y, zp, 1, 1], R3[1, 1])
+            d2p.start()
+
     mix.wait_recv()
     weight_term(x)
+    reduce_1(0, x)
 
     xr0.wait_recv()
     xr2 = put(S_X + 4, OG.at[xp, own_rows], OG.at[xp, own_rows], XN)
     xl0.wait_recv()
     xl2 = put(S_X + 5, OG.at[xn, sib_rows], OG.at[xn, sib_rows], XP)
-
-    for copy in (wa6, wa7, wb6, wb7):
+    reduce_2(0, x)
+
+    for copy in w3:
         copy.wait_recv()
     delta_term(x, True, o)
     delta_term(x, True, c)
+    reduce_3(0, x)
     xr1.wait_recv()
     xl1.wait_recv()
-    for xx in (xp, xn):
-        weight_term(xx)
-        delta_term(xx, False, o)
-        delta_term(xx, False, c)
+    weight_term(xp)
+    reduce_1(1, xp)
+    delta_term(xp, False, o)
+    delta_term(xp, False, c)
+    reduce_4(0, x)
+    weight_term(xn)
+    reduce_1(2, xn)
+    reduce_2(1, xp)
+    delta_term(xn, False, o)
+    delta_term(xn, False, c)
+    reduce_2(2, xn)
+    reduce_3(1, xp)
     xr2.wait_recv()
     xl2.wait_recv()
+
+    ods = []
+    for m in range(2):
+
+        def last_tile(n, _):
+            ms = pl.ds(pl.multiple_of(o * ROWS + m * BLK, BLK), BLK)
+            ns = pl.ds(pl.multiple_of(n * 512, 512), 512)
+            term = dot(OG[xo, ms, :], WB[xo, :, :, :, :, ns].reshape(SPAN, 512))
+            XO[pl.ds(m * BLK, BLK), ns] = (ACC[ms, ns] + term).astype(BF)
+            return 0
+
+        lax.fori_loop(0, 2, last_tile, 0)
+        part = pl.ds(m * BLK, BLK)
+        ods.append(put(S_OD + m, XO.at[part], XI.at[part], SIB))
+    delta_term(xo, False, c)
     weight_term(xo)
-
-    ra0 = put(S_RS + 0, DW.at[:, zo, a_lo], R1.at[0, 0], ZN)
-    ra1 = put(S_RS + 1, DW.at[:, zo, a_hi], R1.at[0, 1], ZP)
-    rb0 = put(S_RS + 8, DW.at[yo, :, b_lo], R1.at[1, 0], YN)
-    rb1 = put(S_RS + 9, DW.at[yo, :, b_hi], R1.at[1, 1], YP)
-
-    delta_term(xo, False, o)
-    XO[...] = ACC[sib_rows, :].astype(BF)
-    od = put(S_OD, XO, XI, SIB)
-    delta_term(xo, False, c)
-    od.wait_recv()
-
-    def norm_back_head(h, _):
+    reduce_1(3, xo)
+    for copy in ods:
+        copy.wait_recv()
+
+    def norm_back_head(h):
         hs = head_cols(h)
         delta = ACC[own_rows, hs] + XI[:, hs].astype(F32)
         scaled = ATT[:, hs]
@@ -362,36 +514,25 @@
         DA[:, hs] = da
         qd = (q[:, hs].astype(F32) * jnp.exp(CC[h])).astype(BF)
         GS[h] = dot_t0(qd, da).astype(BF)
+
+    def first_back(d):
+        p, dev = mate(d)
+        return make(S_B1 + d - 1, GS.at[p], GSI.at[grp], dev)
+
+    def norm_back_step(d, _):
+        norm_back_head(lax.rem(grp + d, 8))
+        first_back(d).start()
         return 0
 
-    lax.fori_loop(0, HEADS, norm_back_head, 0)
-
+    lax.fori_loop(1, 8, norm_back_step, 0)
+    norm_back_head(grp)
     GSI[grp] = GS[grp]
-    b1 = []
-    for d in range(1, 8):
-        p, dev = mate(d)
-        b1.append(put(S_B1 + d - 1, GS.at[p], GSI.at[grp], dev))
-
-    def add_to(target, more):
-        return (target.astype(F32) + more.astype(F32)).astype(BF)
-
-    ra0.wait_recv()
-    for i in range(4):
-        DW[i, zn, a_lo] = add_to(DW[i, zn, a_lo], R1[0, 0, i])
-    ra2 = put(S_RS + 2, DW.at[:, zn, rows_a], R2.at[0, 0], ZN)
-    ra1.wait_recv()
-    for i in range(4):
-        DW[i, zp, a_hi] = add_to(DW[i, zp, a_hi], R1[0, 1, i])
-    ra3 = put(S_RS + 3, DW.at[:, zp, rows_a], R2.at[0, 1], ZP)
-    rb0.wait_recv()
-    for i in range(4):
-        DW[yn, i, b_lo] = add_to(DW[yn, i, b_lo], R1[1, 0, i])
-    rb2 = put(S_RS + 10, DW.at[yn, :, rows_b], R2.at[1, 0], YN)
-    rb1.wait_recv()
-    for i in range(4):
-        DW[yp, i, b_hi] = add_to(DW[yp, i, b_hi], R1[1, 1, i])
-    rb3 = put(S_RS + 11, DW.at[yp, :, rows_b], R2.at[1, 1], YP)
-
+    b1 = [first_back(d) for d in range(1, 8)]
+    live += b1
+
+    reduce_2(3, xo)
+    reduce_3(2, xn)
+    reduce_4(1, xp)
     for copy in b1:
         copy.wait_recv()
 
@@ -456,22 +597,8 @@
 
     lax.fori_loop(4, 8, local_back_head, 0)
 
-    ra2.wait_recv()
-    ra3.wait_recv()
-    for i in range(4):
-        DW[i, z, rows_a] = (
-            DW[i, z, rows_a].astype(F32) + R2[0, 0, i].astype(F32) + R2[0, 1, i].astype(F32)
-        ).astype(BF)
-    ra4 = put(S_RS + 4, DW.at[yo, z, a_lo], R3.at[0, 0], YN)
-    ra5 = put(S_RS + 5, DW.at[yo, z, a_hi], R3.at[0, 1], YP)
-    rb2.wait_recv()
-    rb3.wait_recv()
-    for i in range(4):
-        DW[y, i, rows_b] = (
-            DW[y, i, rows_b].astype(F32) + R2[1, 0, i].astype(F32) + R2[1, 1, i].astype(F32)
-        ).astype(BF)
-    rb4 = put(S_RS + 12, DW.at[y, zo, b_lo], R3.at[1, 0], ZN)
-    rb5 = put(S_RS + 13, DW.at[y, zo, b_hi], R3.at[1, 1], ZP)
+    reduce_3(3, xo)
+    reduce_4(2, xn)
 
     for copy in b3:
         copy.wait_recv()
@@ -486,31 +613,18 @@
 
     lax.fori_loop(0, 4, last_head, 0)
 
-    ra4.wait_recv()
-    DW[yn, z, a_lo] = add_to(DW[yn, z, a_lo], R3[0, 0])
-    ra6 = put(S_RS + 6, DW.at[yn, z, rows_a], R4.at[0, 0], YN)
-    ra5.wait_recv()
-    DW[yp, z, a_hi] = add_to(DW[yp, z, a_hi], R3[0, 1])
-    ra7 = put(S_RS + 7, DW.at[yp, z, rows_a], R4.at[0, 1], YP)
-    rb4.wait_recv()
-    DW[y, zn, b_lo] = add_to(DW[y, zn, b_lo], R3[1, 0])
-    rb6 = put(S_RS + 14, DW.at[y, zn, rows_b], R4.at[1, 0], ZN)
-    rb5.wait_recv()
-    DW[y, zp, b_hi] = add_to(DW[y, zp, b_hi], R3[1, 1])
-    rb7 = put(S_RS + 15, DW.at[y, zp, rows_b], R4.at[1, 1], ZP)
-
+    reduce_4(3, xo)
     lax.fori_loop(4, 8, last_head, 0)
 
-    ra6.wait_recv()
-    ra7.wait_recv()
-    dw[rows_a, :] = (
-        DW[y, z, rows_a].astype(F32) + R4[0, 0].astype(F32) + R4[0, 1].astype(F32)
-    ) * SCALE
-    rb6.wait_recv()
-    rb7.wait_recv()
-    dw[rows_b, :] = (
-        DW[y, z, rows_b].astype(F32) + R4[1, 0].astype(F32) + R4[1, 1].astype(F32)
-    ) * SCALE
+    for half, (from_p, from_n) in enumerate(((c2n, c2p), (d2n, d2p))):
+        from_p.wait_recv()
+        from_n.wait_recv()
+        for i in range(2):
+            dw[pl.ds(half * HALF + i * QUART, QUART), :] = (
+                DW[y, z, half, i].astype(F32)
+                + R4[half, 0, i].astype(F32)
+                + R4[half, 1, i].astype(F32)
+            ) * SCALE
 
     for copy in live:
         copy.wait_send()
@@ -521,16 +635,18 @@
     scratch = [
         vm((4, 2 * ROWS, SPAN), BF),
         vm((ROWS, SPAN), BF),
-        vm((4, 4, UNIT, COLS), BF),
+        vm((4, 4, 2, 2, QUART, COLS), BF),
         vm((2 * ROWS, COLS), F32),
         vm((ROWS, COLS), BF),
         vm((ROWS, COLS), BF),
         vm((2, ROWS, COLS), BF),
-        vm((4, 4, UNIT, COLS), BF),
-        vm((2, 2, 4, QUART, COLS), BF),
-        vm((2, 2, 4, HALF, COLS), BF),
+        vm((4, 4, 2, 2, QUART, COLS), BF),
+        vm((2, 4, QUART, COLS), BF),
+        vm((2, 4, 2, QUART, COLS), BF),
         vm((2, 2, QUART, COLS), BF),
-        vm((2, 2, HALF, COLS), BF),
+        vm((2, 2, 2, QUART, COLS), BF),
+        vm((2, 4, QUART, COLS), BF),
+        vm((2, 4, 2, QUART, COLS), BF),
         vm((HEADS, ROWS, ROWS), BF),
         vm((ROWS, COLS), F32),
         vm((ROWS, COLS), BF),

time: 130 us -> 163 us (1.25); the launches traced: 128 us -> 163 us
  Pallas kernels: 122 us -> 157 us
    pallas_call x1, Pallas kernels: 122 us -> 157 us  [body(): pl.pallas_call(kernel, out_shape=(jax.ShapeDtypeStruct((ROWS, COLS), BF),...]
where the time goes in v1:
time: 163 us
  Pallas kernels  157 us (96%)
  local copies, waits for them, and re-layouts  5.24 us (3%)
    pallas_call x1, Pallas kernels, body(): pl.pallas_call(kernel, out_shape=(jax.ShapeDtypeStruct((ROWS, COLS), BF),...  157 us
    unnamed x10, local copies, waits for them, and re-layouts  5.24 us

profile of v1, /device:TPU:4, one launch (start us, length us, event | category | flops | bytes accessed | tf_op | source)
XLA Modules:
  0.0 163.0 jit_solution(89971960889075750)
XLA Ops:
  0.6 157.1 %shard_map.102 = (bf16[512,1024]{1,0:T(8,128)(2,1)}, bf16[512,1024]{1,0:T(8,128)(2,1)}, bf16[512,1024]{1,0:T(8,128)(2,1)}, f32[192,1024]{1,0:T(8,128)}) custom-call(bf16[512,1024]{1,0:T(8,128)(2,1)} %q.1, bf16[512,1024]{1,0:T(8,128)(2,1)} %k.1, bf16[512,1024]{1,0:T(8,128)(2,1)} %v.1, f32[8,512]{1,0:T(8,128)} %ld.1, f32[1,1024]{1,0:T(1,128)} %bitcast.1, ...), custom_call_target="tpu_custom_call" | custom-call | tf_op jit(solution)/shard_map/pallas_call | solution.py:674
  157.7 0.0 copy-start.1
  157.7 0.0 copy-start
  157.7 2.4 %copy.15 = bf16[512,1024]{1,0:T(8,128)(2,1)} copy(bf16[512,1024]{1,0:T(8,128)(2,1)} %get-tuple-element.8) | data formatting | bytes 2097152
  160.1 0.0 copy-done.1
  160.1 0.0 copy-start.2
  160.1 1.0 copy.16
  161.1 0.0 copy-done
  161.1 1.0 copy.17
  162.1 0.0 copy-done.2
  162.1 0.9 copy.18
Async XLA Ops:
  157.7 2.4 %copy-start.1 = (bf16[512,1024]{1,0:T(8,128)(2,1)S(1)}, bf16[512,1024]{1,0:T(8,128)(2,1)}, u32[]{:S(2)}) copy-start(bf16[512,1024]{1,0:T(8,128)(2,1)} %get-tuple-element.9) | copy-start | bytes 3145732
  157.7 3.4 %copy-start = (bf16[512,1024]{1,0:T(8,128)(2,1)S(1)}, bf16[512,1024]{1,0:T(8,128)(2,1)}, u32[]{:S(2)}) copy-start(bf16[512,1024]{1,0:T(8,128)(2,1)} %get-tuple-element.10) | copy-start | bytes 3145732
  160.1 1.9 %copy-start.2 = (f32[192,1024]{1,0:T(8,128)S(1)}, f32[192,1024]{1,0:T(8,128)}, u32[]{:S(2)}) copy-start(f32[192,1024]{1,0:T(8,128)} %get-tuple-element.11) | copy-start | bytes 2359300

commit v2 on v1

--- a/solution.py
+++ b/solution.py
@@ -30,13 +30,14 @@
 S_A1 = 42
 S_A2 = 50
 S_RS = 58
-S_F1 = 70
-S_F2 = 77
-S_F3 = 80
-S_B1 = 87
-S_B2 = 94
-S_B3 = 97
-S_ALL = 104
+S_E = 70
+S_F1 = 78
+S_F2 = 85
+S_F3 = 88
+S_B1 = 95
+S_B2 = 102
+S_B3 = 105
+S_ALL = 112
 
 
 def dot(a, b):
@@ -54,7 +55,7 @@
 def kernel(
     q, k, v, ld, gain, w, g,
     dq, dk, dv, dw,
-    OG, OGS, WB, ACC, XO, XI, MX, DW, R1, R2, R3, R4, R1B, R2B,
+    OG, OGS, WB, ACC, XO, XI, MX, DW, R1, R2, R3, R4, R1B, R2B, E1, E2, E3, E4,
     PB, ATT, DA, CC, RN, CR,
     ST, STI, RT, RTI, EN, ENT, LL, EP,
     GS, GSI, GR, GRI, GO, GG,
@@ -118,7 +119,10 @@
     own_rows = pl.ds(pl.multiple_of(c * ROWS, ROWS), ROWS)
     sib_rows = pl.ds(pl.multiple_of(o * ROWS, ROWS), ROWS)
 
-    WB[y, z] = w[...].reshape(2, 2, QUART, COLS)
+    half = (pl.ds(0, HALF), pl.ds(HALF, HALF))
+    quart = tuple(tuple(pl.ds(a * HALF + b * QUART, QUART) for b in range(2)) for a in range(2))
+
+    WB[y, z] = w[...]
     wy0 = same(S_W + 0, WB.at[y, z], YN)
     wy1 = same(S_W + 1, WB.at[y, z], YP)
     wz0 = same(S_W + 2, WB.at[y, z], ZN)
@@ -153,7 +157,7 @@
     )
     for h in range(HEADS):
         CR[h] = by_rows[h : h + 1, :]
-        CC[h] = by_cols[:, h : h + 1]
+        CC[h] = jnp.broadcast_to(by_cols[:, h : h + 1], (ROWS, WIDE))
 
     sib.wait_recv()
     xl0 = put(S_X + 2, OG.at[x, sib_rows], OG.at[x, sib_rows], XP)
@@ -165,7 +169,7 @@
     def decays(h, tb, sb):
         cc = CC[h, pl.ds(tb * BLK, BLK), :]
         cr = CR[h, :, pl.ds(sb * BLK, BLK)]
-        grown = jnp.exp(cc - cr)
+        grown = jnp.exp(jnp.concatenate([cc, cc], axis=1) - cr)
         if tb == sb:
             t = lax.broadcasted_iota(jnp.int32, (BLK, BLK), 0)
             s = lax.broadcasted_iota(jnp.int32, (BLK, BLK), 1)
@@ -220,21 +224,21 @@
     live += f1
 
     wy0.wait_recv()
-    wyf0 = same(S_W + 4, WB.at[yp, z, :, 0], YN)
-    wyp0 = same(S_W + 5, WB.at[yp, z, 0], ZN)
-    wyp1 = same(S_W + 6, WB.at[yp, z, 0], ZP)
+    wyf0 = same(S_W + 4, WB.at[yp, z, half[0]], YN)
+    wyp0 = same(S_W + 5, WB.at[yp, z, half[0]], ZN)
+    wyp1 = same(S_W + 6, WB.at[yp, z, half[0]], ZP)
     wy1.wait_recv()
-    wyf1 = same(S_W + 7, WB.at[yn, z, :, 1], YP)
-    wyn0 = same(S_W + 8, WB.at[yn, z, 0], ZN)
-    wyn1 = same(S_W + 9, WB.at[yn, z, 0], ZP)
+    wyf1 = same(S_W + 7, WB.at[yn, z, half[1]], YP)
+    wyn0 = same(S_W + 8, WB.at[yn, z, half[0]], ZN)
+    wyn1 = same(S_W + 9, WB.at[yn, z, half[0]], ZP)
     wz0.wait_recv()
-    wzf0 = same(S_W + 10, WB.at[y, zp, :, 0], ZN)
-    wzp0 = same(S_W + 11, WB.at[y, zp, 1], YN)
-    wzp1 = same(S_W + 12, WB.at[y, zp, 1], YP)
+    wzf0 = same(S_W + 10, WB.at[y, zp, half[0]], ZN)
+    wzp0 = same(S_W + 11, WB.at[y, zp, half[1]], YN)
+    wzp1 = same(S_W + 12, WB.at[y, zp, half[1]], YP)
     wz1.wait_recv()
-    wzf1 = same(S_W + 13, WB.at[y, zn, :, 1], ZP)
-    wzn0 = same(S_W + 14, WB.at[y, zn, 1], YN)
-    wzn1 = same(S_W + 15, WB.at[y, zn, 1], YP)
+    wzf1 = same(S_W + 13, WB.at[y, zn, half[1]], ZP)
+    wzn0 = same(S_W + 14, WB.at[y, zn, half[1]], YN)
+    wzn1 = same(S_W + 15, WB.at[y, zn, half[1]], YP)
 
     for copy in f1:
         copy.wait_recv()
@@ -277,23 +281,23 @@
 
     wyf0.wait_recv()
     wyf1.wait_recv()
-    wyo0 = same(S_W + 16, WB.at[yo, z, 0], ZN)
-    wyo1 = same(S_W + 17, WB.at[yo, z, 0], ZP)
+    wyo0 = same(S_W + 16, WB.at[yo, z, half[0]], ZN)
+    wyo1 = same(S_W + 17, WB.at[yo, z, half[0]], ZP)
     wzf0.wait_recv()
     wzf1.wait_recv()
-    wzo0 = same(S_W + 18, WB.at[y, zo, 1], YN)
-    wzo1 = same(S_W + 19, WB.at[y, zo, 1], YP)
+    wzo0 = same(S_W + 18, WB.at[y, zo, half[1]], YN)
+    wzo1 = same(S_W + 19, WB.at[y, zo, half[1]], YP)
     w3 = []
     for i, (copy, ref, dev) in enumerate(
         (
-            (wyp0, WB.at[yp, zp, 0, 0], ZN),
-            (wyp1, WB.at[yp, zn, 0, 1], ZP),
-            (wzp0, WB.at[yp, zp, 1, 0], YN),
-            (wzp1, WB.at[yn, zp, 1, 1], YP),
-            (wyn0, WB.at[yn, zp, 0, 0], ZN),
-            (wyn1, WB.at[yn, zn, 0, 1], ZP),
-            (wzn0, WB.at[yp, zn, 1, 0], YN),
-            (wzn1, WB.at[yn, zn, 1, 1], YP),
+            (wyp0, WB.at[yp, zp, quart[0][0]], ZN),
+            (wyp1, WB.at[yp, zn, quart[0][1]], ZP),
+            (wzp0, WB.at[yp, zp, quart[1][0]], YN),
+            (wzp1, WB.at[yn, zp, quart[1][1]], YP),
+            (wyn0, WB.at[yn, zp, quart[0][0]], ZN),
+            (wyn1, WB.at[yn, zn, quart[0][1]], ZP),
+            (wzn0, WB.at[yp, zn, quart[1][0]], YN),
+            (wzn1, WB.at[yn, zn, quart[1][1]], YP),
         )
     ):
         copy.wait_recv()
@@ -302,10 +306,15 @@
     for copy in f3:
         copy.wait_recv()
 
+    mean_of = jnp.full((WIDE, WIDE), 1.0 / WIDE, BF)
+
     def attend_head(h, _):
         hs = head_cols(h)
         att = ATT[:, hs] + jnp.exp(CC[h]) * dot(q[:, hs], ENT[h])
-        r = lax.rsqrt(jnp.mean(att * att, axis=-1, keepdims=True) + EPSILON)
+        square = att * att
+        high = square.astype(BF)
+        low = (square - high.astype(F32)).astype(BF)
+        r = lax.rsqrt(dot(high, mean_of) + dot(low, mean_of) + EPSILON)
         scaled = att * r
         ATT[:, hs] = scaled
         RN[h] = r
@@ -317,10 +326,10 @@
 
     for i, (copy, ref, dev) in enumerate(
         (
-            (wyo0, WB.at[yo, zp, 0, 0], ZN),
-            (wyo1, WB.at[yo, zn, 0, 1], ZP),
-            (wzo0, WB.at[yp, zo, 1, 0], YN),
-            (wzo1, WB.at[yn, zo, 1, 1], YP),
+            (wyo0, WB.at[yo, zp, quart[0][0]], ZN),
+            (wyo1, WB.at[yo, zn, quart[0][1]], ZP),
+            (wzo0, WB.at[yp, zo, quart[1][0]], YN),
+            (wzo1, WB.at[yn, zo, quart[1][1]], YP),
         )
     ):
         copy.wait_recv()
@@ -334,9 +343,7 @@
             ns = pl.ds(pl.multiple_of(n * 512, 512), 512)
             term = dot_t0(OG[xx, pl.ds(0, ROWS), ms], MX[0, :, ns])
             term = term + dot_t0(OG[xx, pl.ds(ROWS, ROWS), ms], MX[1, :, ns])
-            DW[xx, pl.ds(2 * pair, 2), :, :, :, ns] = (
-                term.astype(BF).reshape(2, 2, 2, QUART, 512)
-            )
+            DW[xx, pl.ds(2 * pair, 2), :, ns] = term.reshape(2, UNIT, 512).astype(BF)
             return 0
 
         lax.fori_loop(0, 4, tile, 0)
@@ -347,7 +354,7 @@
             n = lax.rem(i, 2)
             ms = pl.ds(pl.multiple_of(half * ROWS + m * BLK, BLK), BLK)
             ns = pl.ds(pl.multiple_of(n * 512, 512), 512)
-            term = dot(OG[xx, ms, :], WB[xx, :, :, :, :, ns].reshape(SPAN, 512))
+            term = dot(OG[xx, ms, :], WB[xx, :, :, ns].reshape(SPAN, 512))
             if first:
                 ACC[ms, ns] = term
             else:
@@ -362,126 +369,166 @@
             total = total + term.astype(F32)
         return total.astype(BF)
 
-    b1lo = make(S_RS + 0, DW.at[yo, :, 1, 0], R1B.at[0], YN)
-    b1hi = make(S_RS + 1, DW.at[yo, :, 1, 1], R1B.at[1], YP)
-    b2n = make(S_RS + 2, DW.at[yn, :, 1], R2B.at[0], YN)
-    b2p = make(S_RS + 3, DW.at[yp, :, 1], R2B.at[1], YP)
-    c1lo = make(S_RS + 4, DW.at[yo, z, 0, 0], R3.at[0, 0], YN)
-    c1hi = make(S_RS + 5, DW.at[yo, z, 0, 1], R3.at[0, 1], YP)
-    c2n = make(S_RS + 6, DW.at[yn, z, 0], R4.at[0, 0], YN)
-    c2p = make(S_RS + 7, DW.at[yp, z, 0], R4.at[0, 1], YP)
-    d1lo = make(S_RS + 8, DW.at[y, zo, 1, 0], R3.at[1, 0], ZN)
-    d1hi = make(S_RS + 9, DW.at[y, zo, 1, 1], R3.at[1, 1], ZP)
-    d2n = make(S_RS + 10, DW.at[y, zn, 1], R4.at[1, 0], ZN)
-    d2p = make(S_RS + 11, DW.at[y, zp, 1], R4.at[1, 1], ZP)
-    live += [b1lo, b1hi, b2n, b2p, c1lo, c1hi, c2n, c2p, d1lo, d1hi, d2n, d2p]
+    early = ((0, x), (1, xp), (2, xn))
+    b1lo = make(S_RS + 0, DW.at[yo, :, quart[1][0]], R1B.at[0], YN)
+    b1hi = make(S_RS + 1, DW.at[yo, :, quart[1][1]], R1B.at[1], YP)
+    b2n = make(S_RS + 2, DW.at[yn, :, half[1]], R2B.at[0], YN)
+    b2p = make(S_RS + 3, DW.at[yp, :, half[1]], R2B.at[1], YP)
+    c1lo = make(S_RS + 4, DW.at[yo, z, quart[0][0]], R3.at[0, 0], YN)
+    c1hi = make(S_RS + 5, DW.at[yo, z, quart[0][1]], R3.at[0, 1], YP)
+    c2n = make(S_RS + 6, DW.at[yn, z, half[0]], R4.at[0, 0], YN)
+    c2p = make(S_RS + 7, DW.at[yp, z, half[0]], R4.at[0, 1], YP)
+    d1lo = make(S_RS + 8, DW.at[y, zo, quart[1][0]], R3.at[1, 0], ZN)
+    d1hi = make(S_RS + 9, DW.at[y, zo, quart[1][1]], R3.at[1, 1], ZP)
+    d2n = make(S_RS + 10, DW.at[y, zn, half[1]], R4.at[1, 0], ZN)
+    d2p = make(S_RS + 11, DW.at[y, zp, half[1]], R4.at[1, 1], ZP)
+    e1lo = make(S_E + 0, DW.at[xo, zo, half[0]], E1.at[0], ZN)
+    e1hi = make(S_E + 1, DW.at[xo, zo, half[1]], E1.at[1], ZP)
+    e2n = make(S_E + 2, DW.at[xo, zn], E2.at[0], ZN)
+    e2p = make(S_E + 3, DW.at[xo, zp], E2.at[1], ZP)
+    f1lo = make(S_E + 4, DW.at[xo, z, half[0]], E3.at[0], YN)
+    f1hi = make(S_E + 5, DW.at[xo, z, half[1]], E3.at[1], YP)
+    f2n = make(S_E + 6, DW.at[xo, z], E4.at[0], YN)
+    f2p = make(S_E + 7, DW.at[xo, z], E4.at[1], YP)
+    live += [e1lo, e1hi, e2n, e2p]
     a1 = {}
     a2 = {}
 
-    def reduce_1(j, xx):
+    def first_hop(j, xx):
         a1[j] = (
-            put(S_A1 + 2 * j, DW.at[xx, zo, 0, 0], R1.at[0, j], ZN),
-            put(S_A1 + 2 * j + 1, DW.at[xx, zo, 0, 1], R1.at[1, j], ZP),
+            put(S_A1 + 2 * j, DW.at[xx, zo, quart[0][0]], R1.at[0, j], ZN),
+            put(S_A1 + 2 * j + 1, DW.at[xx, zo, quart[0][1]], R1.at[1, j], ZP),
         )
 
-        @pl.when(xx == yo)
+    def first_hop_y():
+        @pl.when(yo != xo)
         def _():
             b1lo.start()
             b1hi.start()
 
-    def reduce_2(j, xx):
-        a1[j][0].wait_recv()
-        DW[xx, zn, 0, 0] = add_to(DW[xx, zn, 0, 0], R1[0, j])
-        to_n = put(S_A2 + 2 * j, DW.at[xx, zn, 0], R2.at[0, j], ZN)
-        a1[j][1].wait_recv()
-        DW[xx, zp, 0, 1] = add_to(DW[xx, zp, 0, 1], R1[1, j])
-        to_p = put(S_A2 + 2 * j + 1, DW.at[xx, zp, 0], R2.at[1, j], ZP)
-        a2[j] = (to_n, to_p)
-
-        @pl.when(xx == yn)
+    def second_hop():
+        for j, xx in early:
+            a1[j][0].wait_recv()
+            DW[xx, zn, quart[0][0]] = add_to(DW[xx, zn, quart[0][0]], R1[0, j])
+            to_n = put(S_A2 + 2 * j, DW.at[xx, zn, half[0]], R2.at[0, j], ZN)
+            a1[j][1].wait_recv()
+            DW[xx, zp, quart[0][1]] = add_to(DW[xx, zp, quart[0][1]], R1[1, j])
+            to_p = put(S_A2 + 2 * j + 1, DW.at[xx, zp, half[0]], R2.at[1, j], ZP)
+            a2[j] = (to_n, to_p)
+
+        @pl.when(yn != xo)
         def _():
             b1lo.wait_recv()
             for i in range(4):
-                DW[yn, i, 1, 0] = add_to(DW[yn, i, 1, 0], R1B[0, i])
+                DW[yn, i, quart[1][0]] = add_to(DW[yn, i, quart[1][0]], R1B[0, i])
             b2n.start()
 
-        @pl.when(xx == yp)
+        @pl.when(yp != xo)
         def _():
             b1hi.wait_recv()
             for i in range(4):
-                DW[yp, i, 1, 1] = add_to(DW[yp, i, 1, 1], R1B[1, i])
+                DW[yp, i, quart[1][1]] = add_to(DW[yp, i, quart[1][1]], R1B[1, i])
             b2p.start()
 
-    def reduce_3(j, xx):
-        a2[j][0].wait_recv()
-        a2[j][1].wait_recv()
-        DW[xx, z, 0] = add_to(DW[xx, z, 0], R2[0, j], R2[1, j])
-
-        @pl.when(xx == yo)
+    def third_hop():
+        for j, xx in early:
+            a2[j][0].wait_recv()
+            a2[j][1].wait_recv()
+            DW[xx, z, half[0]] = add_to(DW[xx, z, half[0]], R2[0, j], R2[1, j])
+
+        @pl.when(yo != xo)
         def _():
             c1lo.start()
             c1hi.start()
 
-        @pl.when(xx == y)
+        @pl.when(y != xo)
         def _():
             b2n.wait_recv()
             b2p.wait_recv()
             for i in range(4):
-                DW[y, i, 1] = add_to(DW[y, i, 1], R2B[0, i], R2B[1, i])
+                DW[y, i, half[1]] = add_to(DW[y, i, half[1]], R2B[0, i], R2B[1, i])
             d1lo.start()
             d1hi.start()
 
-    def reduce_4(j, xx):
-        @pl.when(xx == yn)
+    def fourth_hop():
+        @pl.when(yn != xo)
         def _():
             c1lo.wait_recv()
-            DW[yn, z, 0, 0] = add_to(DW[yn, z, 0, 0], R3[0, 0])
+            DW[yn, z, quart[0][0]] = add_to(DW[yn, z, quart[0][0]], R3[0, 0])
             c2n.start()
 
-        @pl.when(xx == yp)
+        @pl.when(yp != xo)
         def _():
             c1hi.wait_recv()
-            DW[yp, z, 0, 1] = add_to(DW[yp, z, 0, 1], R3[0, 1])
+            DW[yp, z, quart[0][1]] = add_to(DW[yp, z, quart[0][1]], R3[0, 1])
             c2p.start()
 
-        @pl.when(xx == y)
+        @pl.when(y != xo)
         def _():
             d1lo.wait_recv()
-            DW[y, zn, 1, 0] = add_to(DW[y, zn, 1, 0], R3[1, 0])
+            DW[y, zn, quart[1][0]] = add_to(DW[y, zn, quart[1][0]], R3[1, 0])
             d2n.start()
             d1hi.wait_recv()
-            DW[y, zp, 1, 1] = add_to(DW[y, zp, 1, 1], R3[1, 1])
+            DW[y, zp, quart[1][1]] = add_to(DW[y, zp, quart[1][1]], R3[1, 1])
             d2p.start()
+
+    def late_second_hop():
+        e1lo.wait_recv()
+        DW[xo, zn, half[0]] = add_to(DW[xo, zn, half[0]], E1[0])
+        e2n.start()
+        e1hi.wait_recv()
+        DW[xo, zp, half[1]] = add_to(DW[xo, zp, half[1]], E1[1])
+        e2p.start()
+
+    def late_third_hop():
+        e2n.wait_recv()
+        e2p.wait_recv()
+        for i in range(2):
+            DW[xo, z, half[i]] = add_to(DW[xo, z, half[i]], E2[0, half[i]], E2[1, half[i]])
+
+        @pl.when(yo == xo)
+        def _():
+            f1lo.start()
+            f1hi.start()
+
+    def late_fourth_hop():
+        @pl.when(yn == xo)
+        def _():
+            f1lo.wait_recv()
+            DW[xo, z, half[0]] = add_to(DW[xo, z, half[0]], E3[0])
+            f2n.start()
+
+        @pl.when(yp == xo)
+        def _():
+            f1hi.wait_recv()
+            DW[xo, z, half[1]] = add_to(DW[xo, z, half[1]], E3[1])
+            f2p.start()
 
     mix.wait_recv()
     weight_term(x)
-    reduce_1(0, x)
+    first_hop(0, x)
 
     xr0.wait_recv()
     xr2 = put(S_X + 4, OG.at[xp, own_rows], OG.at[xp, own_rows], XN)
     xl0.wait_recv()
     xl2 = put(S_X + 5, OG.at[xn, sib_rows], OG.at[xn, sib_rows], XP)
-    reduce_2(0, x)
+    xr1.wait_recv()
+    weight_term(xp)
+    first_hop(1, xp)
+    xl1.wait_recv()
+    weight_term(xn)
+    first_hop(2, xn)
+    first_hop_y()
 
     for copy in w3:
         copy.wait_recv()
     delta_term(x, True, o)
     delta_term(x, True, c)
-    reduce_3(0, x)
-    xr1.wait_recv()
-    xl1.wait_recv()
-    weight_term(xp)
-    reduce_1(1, xp)
     delta_term(xp, False, o)
     delta_term(xp, False, c)
-    reduce_4(0, x)
-    weight_term(xn)
-    reduce_1(2, xn)
-    reduce_2(1, xp)
+    second_hop()
     delta_term(xn, False, o)
     delta_term(xn, False, c)
-    reduce_2(2, xn)
-    reduce_3(1, xp)
     xr2.wait_recv()
     xl2.wait_recv()
 
@@ -491,7 +538,7 @@
         def last_tile(n, _):
             ms = pl.ds(pl.multiple_of(o * ROWS + m * BLK, BLK), BLK)
             ns = pl.ds(pl.multiple_of(n * 512, 512), 512)
-            term = dot(OG[xo, ms, :], WB[xo, :, :, :, :, ns].reshape(SPAN, 512))
+            term = dot(OG[xo, ms, :], WB[xo, :, :, ns].reshape(SPAN, 512))
             XO[pl.ds(m * BLK, BLK), ns] = (ACC[ms, ns] + term).astype(BF)
             return 0
 
@@ -500,7 +547,8 @@
         ods.append(put(S_OD + m, XO.at[part], XI.at[part], SIB))
     delta_term(xo, False, c)
     weight_term(xo)
-    reduce_1(3, xo)
+    e1lo.start()
+    e1hi.start()
     for copy in ods:
         copy.wait_recv()
 
@@ -509,7 +557,7 @@
         delta = ACC[own_rows, hs] + XI[:, hs].astype(F32)
         scaled = ATT[:, hs]
         gg = delta * gain[:, hs]
-        da = RN[h] * (gg - scaled * jnp.mean(gg * scaled, axis=-1, keepdims=True))
+        da = RN[h] * (gg - scaled * dot((gg * scaled).astype(BF), mean_of))
         da = da.astype(BF)
         DA[:, hs] = da
         qd = (q[:, hs].astype(F32) * jnp.exp(CC[h])).astype(BF)
@@ -530,9 +578,7 @@
     b1 = [first_back(d) for d in range(1, 8)]
     live += b1
 
-    reduce_2(3, xo)
-    reduce_3(2, xn)
-    reduce_4(1, xp)
+    third_hop()
     for copy in b1:
         copy.wait_recv()
 
@@ -574,6 +620,7 @@
             ACC[blk(2 + sb), hs] = dv_blk[sb]
         return 0
 
+    late_second_hop()
     lax.fori_loop(0, 4, local_back_head, 0)
 
     for copy in b2:
@@ -595,39 +642,79 @@
         p, dev = mate(d)
         b3.append(put(S_B3 + d - 1, GO.at[p], GG.at[grp], dev))
 
+    fourth_hop()
     lax.fori_loop(4, 8, local_back_head, 0)
-
-    reduce_3(3, xo)
-    reduce_4(2, xn)
-
-    for copy in b3:
-        copy.wait_recv()
-
-    def last_head(h, _):
+    late_third_hop()
+
+    def last_head(h):
         hs = head_cols(h)
         total = CR[h, :, pl.ds(ROWS - WIDE, WIDE)][:, WIDE - 1 : WIDE]
         tail = jnp.exp(total - CC[h])
         dk[:, hs] = (ACC[pl.ds(0, ROWS), hs] + tail * dot_t1(v[:, hs], GG[h])).astype(BF)
         dv[:, hs] = (ACC[pl.ds(ROWS, ROWS), hs] + tail * dot(k[:, hs], GG[h])).astype(BF)
+
+    last_head(grp)
+
+    def last_step(d, _):
+        p = lax.rem(grp + 8 - d, 8)
+        make(S_B3 + d - 1, GO.at[p], GG.at[grp], SIB).wait_recv()
+        last_head(p)
         return 0
 
-    lax.fori_loop(0, 4, last_head, 0)
-
-    reduce_4(3, xo)
-    lax.fori_loop(4, 8, last_head, 0)
-
-    for half, (from_p, from_n) in enumerate(((c2n, c2p), (d2n, d2p))):
-        from_p.wait_recv()
-        from_n.wait_recv()
+    lax.fori_loop(1, 4, last_step, 0)
+    late_fourth_hop()
+    lax.fori_loop(4, 8, last_step, 0)
+
+    @pl.when(y != xo)
+    def _():
+        for i, (from_p, from_n) in enumerate(((c2n, c2p), (d2n, d2p))):
+            from_p.wait_recv()
+            from_n.wait_recv()
+            dw[half[i], :] = (
+                DW[y, z, half[i]].astype(F32) + R4[i, 0].astype(F32) + R4[i, 1].astype(F32)
+            ) * SCALE
+
+    @pl.when(y == xo)
+    def _():
+        f2n.wait_recv()
+        f2p.wait_recv()
         for i in range(2):
-            dw[pl.ds(half * HALF + i * QUART, QUART), :] = (
-                DW[y, z, half, i].astype(F32)
-                + R4[half, 0, i].astype(F32)
-                + R4[half, 1, i].astype(F32)
+            dw[half[i], :] = (
+                DW[y, z, half[i]].astype(F32)
+                + E4[0, half[i]].astype(F32)
+                + E4[1, half[i]].astype(F32)
             ) * SCALE
+
+    for place, copies in (
+        (yo, (b1lo, b1hi, c1lo, c1hi)),
+        (yn, (b2n, c2n)),
+        (yp, (b2p, c2p)),
+        (y, (d1lo, d1hi, d2n, d2p)),
+    ):
+
+        @pl.when(place != xo)
+        def _():
+            for copy in copies:
+                copy.wait_send()
+
+    for place, copies in ((yo, (f1lo, f1hi)), (yn, (f2n,)), (yp, (f2p,))):
+
+        @pl.when(place == xo)
+        def _():
+            for copy in copies:
+                copy.wait_send()
 
     for copy in live:
         copy.wait_send()
+
+
+def hand_over(a, b, c, d, to_a, to_b, to_c, to_d, sems):
+    pairs = ((a, to_a), (b, to_b), (c, to_c), (d, to_d))
+    copies = [pltpu.make_async_copy(s, t, sems.at[i]) for i, (s, t) in enumerate(pairs)]
+    for copy in copies:
+        copy.start()
+    for copy in copies:
+        copy.wait()
 
 
 def body(query_rows, key_rows, value_rows, log_decay, norm_gain, out_weight, out_grad):
@@ -635,23 +722,27 @@
     scratch = [
         vm((4, 2 * ROWS, SPAN), BF),
         vm((ROWS, SPAN), BF),
-        vm((4, 4, 2, 2, QUART, COLS), BF),
+        vm((4, 4, UNIT, COLS), BF),
         vm((2 * ROWS, COLS), F32),
         vm((ROWS, COLS), BF),
         vm((ROWS, COLS), BF),
         vm((2, ROWS, COLS), BF),
-        vm((4, 4, 2, 2, QUART, COLS), BF),
+        vm((4, 4, UNIT, COLS), BF),
+        vm((2, 3, QUART, COLS), BF),
+        vm((2, 3, HALF, COLS), BF),
+        vm((2, 2, QUART, COLS), BF),
+        vm((2, 2, HALF, COLS), BF),
         vm((2, 4, QUART, COLS), BF),
-        vm((2, 4, 2, QUART, COLS), BF),
-        vm((2, 2, QUART, COLS), BF),
-        vm((2, 2, 2, QUART, COLS), BF),
-        vm((2, 4, QUART, COLS), BF),
-        vm((2, 4, 2, QUART, COLS), BF),
+        vm((2, 4, HALF, COLS), BF),
+        vm((2, HALF, COLS), BF),
+        vm((2, UNIT, COLS), BF),
+        vm((2, HALF, COLS), BF),
+        vm((2, UNIT, COLS), BF),
         vm((HEADS, ROWS, ROWS), BF),
         vm((ROWS, COLS), F32),
         vm((ROWS, COLS), BF),
-        vm((HEADS, ROWS, 1), F32),
-        vm((HEADS, ROWS, 1), F32),
+        vm((HEADS, ROWS, WIDE), F32),
+        vm((HEADS, ROWS, WIDE), F32),
         vm((HEADS, 1, ROWS), F32),
         vm((8, WIDE + 16, WIDE), BF),
         vm((8, WIDE + 16, WIDE), BF),
@@ -671,14 +762,15 @@
         pltpu.SemaphoreType.DMA((S_ALL,)),
     ]
     spec = pl.BlockSpec(memory_space=pltpu.VMEM)
-    return pl.pallas_call(
+    shapes = (
+        jax.ShapeDtypeStruct((ROWS, COLS), BF),
+        jax.ShapeDtypeStruct((ROWS, COLS), BF),
+        jax.ShapeDtypeStruct((ROWS, COLS), BF),
+        jax.ShapeDtypeStruct((UNIT, COLS), F32),
+    )
+    results = pl.pallas_call(
         kernel,
-        out_shape=(
-            jax.ShapeDtypeStruct((ROWS, COLS), BF),
-            jax.ShapeDtypeStruct((ROWS, COLS), BF),
-            jax.ShapeDtypeStruct((ROWS, COLS), BF),
-            jax.ShapeDtypeStruct((UNIT, COLS), F32),
-        ),
+        out_shape=shapes,
         in_specs=[spec] * 7,
         out_specs=(spec,) * 4,
         scratch_shapes=scratch,
@@ -694,6 +786,14 @@
         out_weight,
         out_grad,
     )
+    anywhere = pl.BlockSpec(memory_space=pl.ANY)
+    return pl.pallas_call(
+        hand_over,
+        out_shape=shapes,
+        in_specs=[anywhere] * 4,
+        out_specs=(anywhere,) * 4,
+        scratch_shapes=[pltpu.SemaphoreType.DMA((4,))],
+    )(*results)
 
 
 def solution(mesh):

time: 163 us -> 235 us (1.44)
  Pallas kernels: 157 us -> 235 us
  local copies, waits for them, and re-layouts: 5.24 us -> 0 us
    pallas_call x1 -> x2, Pallas kernels: 157 us -> 235 us  [the longest x1 120 us: body(): pl.pallas_call(hand_over, out_shape=shapes, in_specs=[anywhere] * 4, out_...]
    unnamed x10 -> x0, local copies, waits for them, and re-layouts: 5.24 us -> none
where the time goes in v2:
time: 235 us
  Pallas kernels  235 us (100%)
    pallas_call x1, Pallas kernels, body(): pl.pallas_call(hand_over, out_shape=shapes, in_specs=[anywhere] * 4, out_...  120 us
    pallas_call x1, Pallas kernels, body(): pl.pallas_call(kernel, out_shape=shapes, in_specs=[spec] * 7, out_specs=(...  114 us

profile of v2, /device:TPU:4, one launch (start us, length us, event | category | flops | bytes accessed | tf_op | source)
XLA Modules:
  0.0 235.1 jit_solution(18248340940009332988)
XLA Ops:
  0.6 114.3 %shard_map.102 = (bf16[512,1024]{1,0:T(8,128)(2,1)}, bf16[512,1024]{1,0:T(8,128)(2,1)}, bf16[512,1024]{1,0:T(8,128)(2,1)}, f32[192,1024]{1,0:T(8,128)}) custom-call(bf16[512,1024]{1,0:T(8,128)(2,1)} %q.1, bf16[512,1024]{1,0:T(8,128)(2,1)} %k.1, bf16[512,1024]{1,0:T(8,128)(2,1)} %v.1, f32[8,512]{1,0:T(8,128)} %ld.1, f32[1,1024]{1,0:T(1,128)} %bitcast.1, ...), custom_call_target="tpu_custom_call" | custom-call | tf_op jit(solution)/shard_map/pallas_call | solution.py:771
  114.9 120.3 %shard_map.103 = (bf16[512,1024]{1,0:T(8,128)(2,1)}, bf16[512,1024]{1,0:T(8,128)(2,1)}, bf16[512,1024]{1,0:T(8,128)(2,1)}, f32[192,1024]{1,0:T(8,128)}) custom-call(bf16[512,1024]{1,0:T(8,128)(2,1)} %get-tuple-element.8.a, bf16[512,1024]{1,0:T(8,128)(2,1)} %get-tuple-element.9.b, bf16[512,1024]{1,0:T(8,128)(2,1)} %get-tuple-element.10.c, ...), custom_call_target="tpu_custom_call" | custom-call | tf_op jit(solution)/shard_map/pallas_call | solution.py:790

commit v3 on v2

--- a/solution.py
+++ b/solution.py
@@ -56,7 +56,7 @@
     q, k, v, ld, gain, w, g,
     dq, dk, dv, dw,
     OG, OGS, WB, ACC, XO, XI, MX, DW, R1, R2, R3, R4, R1B, R2B, E1, E2, E3, E4,
-    PB, ATT, DA, CC, RN, CR,
+    PB, ATT, DA, DL, CC, RN, CR,
     ST, STI, RT, RTI, EN, ENT, LL, EP,
     GS, GSI, GR, GRI, GO, GG,
     ss, rs,
@@ -308,13 +308,18 @@
 
     mean_of = jnp.full((WIDE, WIDE), 1.0 / WIDE, BF)
 
+    def halves(a):
+        high = a.astype(BF)
+        return high, (a - high.astype(F32)).astype(BF)
+
+    def row_mean(a):
+        high, low = halves(a)
+        return dot(high, mean_of) + dot(low, mean_of)
+
     def attend_head(h, _):
         hs = head_cols(h)
         att = ATT[:, hs] + jnp.exp(CC[h]) * dot(q[:, hs], ENT[h])
-        square = att * att
-        high = square.astype(BF)
-        low = (square - high.astype(F32)).astype(BF)
-        r = lax.rsqrt(dot(high, mean_of) + dot(low, mean_of) + EPSILON)
+        r = lax.rsqrt(row_mean(att * att) + EPSILON)
         scaled = att * r
         ATT[:, hs] = scaled
         RN[h] = r
@@ -349,12 +354,10 @@
         lax.fori_loop(0, 4, tile, 0)
 
     def delta_term(xx, first, half):
-        def tile(i, _):
-            m = lax.div(i, 2)
-            n = lax.rem(i, 2)
-            ms = pl.ds(pl.multiple_of(half * ROWS + m * BLK, BLK), BLK)
-            ns = pl.ds(pl.multiple_of(n * 512, 512), 512)
-            term = dot(OG[xx, ms, :], WB[xx, :, :, ns].reshape(SPAN, 512))
+        def tile(n, _):
+            ms = pl.ds(pl.multiple_of(half * ROWS, ROWS), ROWS)
+            ns = pl.ds(pl.multiple_of(n * 256, 256), 256)
+            term = dot(OG[xx, ms, :], WB[xx, :, :, ns].reshape(SPAN, 256))
             if first:
                 ACC[ms, ns] = term
             else:
@@ -532,23 +535,22 @@
     xr2.wait_recv()
     xl2.wait_recv()
 
-    ods = []
-    for m in range(2):
-
-        def last_tile(n, _):
-            ms = pl.ds(pl.multiple_of(o * ROWS + m * BLK, BLK), BLK)
-            ns = pl.ds(pl.multiple_of(n * 512, 512), 512)
-            term = dot(OG[xo, ms, :], WB[xo, :, :, ns].reshape(SPAN, 512))
-            XO[pl.ds(m * BLK, BLK), ns] = (ACC[ms, ns] + term).astype(BF)
-            return 0
-
-        lax.fori_loop(0, 2, last_tile, 0)
-        part = pl.ds(m * BLK, BLK)
-        ods.append(put(S_OD + m, XO.at[part], XI.at[part], SIB))
-    delta_term(xo, False, c)
     weight_term(xo)
     e1lo.start()
     e1hi.start()
+    ods = []
+    for m in range(2):
+
+        def last_tile(n, _):
+            ns = pl.ds(pl.multiple_of(n * 256, 256), 256)
+            term = dot(OG[xo, sib_rows, :], WB[xo, :, :, ns].reshape(SPAN, 256))
+            XO[:, ns] = (ACC[sib_rows, ns] + term).astype(BF)
+            return 0
+
+        lax.fori_loop(2 * m, 2 * m + 2, last_tile, 0)
+        part = pl.ds(m * ROWS, ROWS)
+        ods.append(put(S_OD + m, XO.at[:, part], XI.at[:, part], SIB))
+    delta_term(xo, False, c)
     for copy in ods:
         copy.wait_recv()
 
@@ -557,9 +559,10 @@
         delta = ACC[own_rows, hs] + XI[:, hs].astype(F32)
         scaled = ATT[:, hs]
         gg = delta * gain[:, hs]
-        da = RN[h] * (gg - scaled * dot((gg * scaled).astype(BF), mean_of))
-        da = da.astype(BF)
+        da = RN[h] * (gg - scaled * row_mean(gg * scaled))
+        da, low = halves(da)
         DA[:, hs] = da
+        DL[:, hs] = low
         qd = (q[:, hs].astype(F32) * jnp.exp(CC[h])).astype(BF)
         GS[h] = dot_t0(qd, da).astype(BF)
 
@@ -578,7 +581,7 @@
     b1 = [first_back(d) for d in range(1, 8)]
     live += b1
 
-    third_hop()
+    late_second_hop()
     for copy in b1:
         copy.wait_recv()
 
@@ -608,7 +611,9 @@
             da = DA[blk(tb), hs]
             out = jnp.exp(CC[h, blk(tb), :]) * dot_t1(da, ENT[h])
             for sb in range(tb + 1):
-                dp = (dot_t1(da, v[blk(sb), hs]) * decays(h, tb, sb)).astype(BF)
+                vs = v[blk(sb), hs]
+                dp = dot_t1(da, vs) + dot_t1(DL[blk(tb), hs], vs)
+                dp = (dp * decays(h, tb, sb)).astype(BF)
                 out = out + dot(dp, k[blk(sb), hs])
                 k_term = dot_t0(dp, q[blk(tb), hs])
                 v_term = dot_t0(PB[h, blk(tb), blk(sb)], da)
@@ -620,9 +625,9 @@
             ACC[blk(2 + sb), hs] = dv_blk[sb]
         return 0
 
-    late_second_hop()
     lax.fori_loop(0, 4, local_back_head, 0)
 
+    third_hop()
     for copy in b2:
         copy.wait_recv()
     carried_back = jnp.zeros((WIDE, WIDE), F32)
@@ -642,9 +647,8 @@
         p, dev = mate(d)
         b3.append(put(S_B3 + d - 1, GO.at[p], GG.at[grp], dev))
 
-    fourth_hop()
+    late_third_hop()
     lax.fori_loop(4, 8, local_back_head, 0)
-    late_third_hop()
 
     def last_head(h):
         hs = head_cols(h)
@@ -653,6 +657,7 @@
         dk[:, hs] = (ACC[pl.ds(0, ROWS), hs] + tail * dot_t1(v[:, hs], GG[h])).astype(BF)
         dv[:, hs] = (ACC[pl.ds(ROWS, ROWS), hs] + tail * dot(k[:, hs], GG[h])).astype(BF)
 
+    fourth_hop()
     last_head(grp)
 
     def last_step(d, _):
@@ -661,8 +666,8 @@
         last_head(p)
         return 0
 
+    late_fourth_hop()
     lax.fori_loop(1, 4, last_step, 0)
-    late_fourth_hop()
     lax.fori_loop(4, 8, last_step, 0)
 
     @pl.when(y != xo)
@@ -706,15 +711,6 @@
 
     for copy in live:
         copy.wait_send()
-
-
-def hand_over(a, b, c, d, to_a, to_b, to_c, to_d, sems):
-    pairs = ((a, to_a), (b, to_b), (c, to_c), (d, to_d))
-    copies = [pltpu.make_async_copy(s, t, sems.at[i]) for i, (s, t) in enumerate(pairs)]
-    for copy in copies:
-        copy.start()
-    for copy in copies:
-        copy.wait()
 
 
 def body(query_rows, key_rows, value_rows, log_decay, norm_gain, out_weight, out_grad):
@@ -740,6 +736,7 @@
         vm((2, UNIT, COLS), BF),
         vm((HEADS, ROWS, ROWS), BF),
         vm((ROWS, COLS), F32),
+        vm((ROWS, COLS), BF),
         vm((ROWS, COLS), BF),
         vm((HEADS, ROWS, WIDE), F32),
         vm((HEADS, ROWS, WIDE), F32),
@@ -768,7 +765,7 @@
         jax.ShapeDtypeStruct((ROWS, COLS), BF),
         jax.ShapeDtypeStruct((UNIT, COLS), F32),
     )
-    results = pl.pallas_call(
+    return pl.pallas_call(
         kernel,
         out_shape=shapes,
         in_specs=[spec] * 7,
@@ -786,14 +783,6 @@
         out_weight,
         out_grad,
     )
-    anywhere = pl.BlockSpec(memory_space=pl.ANY)
-    return pl.pallas_call(
-        hand_over,
-        out_shape=shapes,
-        in_specs=[anywhere] * 4,
-        out_specs=(anywhere,) * 4,
-        scratch_shapes=[pltpu.SemaphoreType.DMA((4,))],
-    )(*results)
 
 
 def solution(mesh):

time: 235 us -> 117 us (0.50)
  Pallas kernels: 235 us -> 111 us
  local copies, waits for them, and re-layouts: 0 us -> 5.24 us
    pallas_call x1 -> x0, Pallas kernels: 120 us -> none  [body(): pl.pallas_call(hand_over, out_shape=shapes, in_specs=[anywhere] * 4, out_...]
    unnamed x0 -> x10, local copies, waits for them, and re-layouts: none -> 5.24 us
    pallas_call x1, Pallas kernels: 114 us -> 111 us  [body(): pl.pallas_call(kernel, out_shape=shapes, in_specs=[spec] * 7, out_specs=(...]
where the time goes in v3:
time: 117 us
  Pallas kernels  111 us (95%)
  local copies, waits for them, and re-layouts  5.24 us (4%)
    pallas_call x1, Pallas kernels, body(): pl.pallas_call(kernel, out_shape=shapes, in_specs=[spec] * 7, out_specs=(...  111 us
    unnamed x10, local copies, waits for them, and re-layouts  5.24 us

profile of v3, /device:TPU:4, one launch (start us, length us, event | category | flops | bytes accessed | tf_op | source)
XLA Modules:
  0.0 116.6 jit_solution(10958611125679868647)
XLA Ops:
  0.6 110.7 %shard_map.102 = (bf16[512,1024]{1,0:T(8,128)(2,1)}, bf16[512,1024]{1,0:T(8,128)(2,1)}, bf16[512,1024]{1,0:T(8,128)(2,1)}, f32[192,1024]{1,0:T(8,128)}) custom-call(bf16[512,1024]{1,0:T(8,128)(2,1)} %q.1, bf16[512,1024]{1,0:T(8,128)(2,1)} %k.1, bf16[512,1024]{1,0:T(8,128)(2,1)} %v.1, f32[8,512]{1,0:T(8,128)} %ld.1, f32[1,1024]{1,0:T(1,128)} %bitcast.1, ...), custom_call_target="tpu_custom_call" | custom-call | tf_op jit(solution)/shard_map/pallas_call | solution.py:768
  111.3 0.0 copy-start.1
  111.3 0.0 copy-start
  111.3 2.4 %copy.15 = bf16[512,1024]{1,0:T(8,128)(2,1)} copy(bf16[512,1024]{1,0:T(8,128)(2,1)} %get-tuple-element.8) | data formatting | bytes 2097152
  113.8 0.0 copy-done.1
  113.8 0.0 copy-start.2
  113.8 1.0 copy.16
  114.7 0.0 copy-done
  114.7 1.0 copy.17
  115.7 0.0 copy-done.2
  115.7 0.9 copy.18
Async XLA Ops:
  111.3 2.4 %copy-start.1 = (bf16[512,1024]{1,0:T(8,128)(2,1)S(1)}, bf16[512,1024]{1,0:T(8,128)(2,1)}, u32[]{:S(2)}) copy-start(bf16[512,1024]{1,0:T(8,128)(2,1)} %get-tuple-element.9) | copy-start | bytes 3145732
  111.3 3.4 %copy-start = (bf16[512,1024]{1,0:T(8,128)(2,1)S(1)}, bf16[512,1024]{1,0:T(8,128)(2,1)}, u32[]{:S(2)}) copy-start(bf16[512,1024]{1,0:T(8,128)(2,1)} %get-tuple-element.10) | copy-start | bytes 3145732
  113.8 1.9 %copy-start.2 = (f32[192,1024]{1,0:T(8,128)S(1)}, f32[192,1024]{1,0:T(8,128)}, u32[]{:S(2)}) copy-start(f32[192,1024]{1,0:T(8,128)} %get-tuple-element.11) | copy-start | bytes 2359300

commit v4 on v3

--- a/solution.py
+++ b/solution.py
@@ -403,8 +403,8 @@
             put(S_A1 + 2 * j + 1, DW.at[xx, zo, quart[0][1]], R1.at[1, j], ZP),
         )
 
-    def first_hop_y():
-        @pl.when(yo != xo)
+    def first_hop_y(xx):
+        @pl.when(yo == xx)
         def _():
             b1lo.start()
             b1hi.start()
@@ -419,6 +419,7 @@
             to_p = put(S_A2 + 2 * j + 1, DW.at[xx, zp, half[0]], R2.at[1, j], ZP)
             a2[j] = (to_n, to_p)
 
+    def second_hop_y():
         @pl.when(yn != xo)
         def _():
             b1lo.wait_recv()
@@ -444,6 +445,7 @@
             c1lo.start()
             c1hi.start()
 
+    def third_hop_y():
         @pl.when(y != xo)
         def _():
             b2n.wait_recv()
@@ -510,6 +512,7 @@
     mix.wait_recv()
     weight_term(x)
     first_hop(0, x)
+    first_hop_y(x)
 
     xr0.wait_recv()
     xr2 = put(S_X + 4, OG.at[xp, own_rows], OG.at[xp, own_rows], XN)
@@ -518,18 +521,20 @@
     xr1.wait_recv()
     weight_term(xp)
     first_hop(1, xp)
+    first_hop_y(xp)
     xl1.wait_recv()
     weight_term(xn)
     first_hop(2, xn)
-    first_hop_y()
+    first_hop_y(xn)
 
     for copy in w3:
         copy.wait_recv()
     delta_term(x, True, o)
     delta_term(x, True, c)
+    second_hop()
     delta_term(xp, False, o)
     delta_term(xp, False, c)
-    second_hop()
+    second_hop_y()
     delta_term(xn, False, o)
     delta_term(xn, False, c)
     xr2.wait_recv()
@@ -551,6 +556,7 @@
         part = pl.ds(m * ROWS, ROWS)
         ods.append(put(S_OD + m, XO.at[:, part], XI.at[:, part], SIB))
     delta_term(xo, False, c)
+    third_hop()
     for copy in ods:
         copy.wait_recv()
 
@@ -627,7 +633,7 @@
 
     lax.fori_loop(0, 4, local_back_head, 0)
 
-    third_hop()
+    third_hop_y()
     for copy in b2:
         copy.wait_recv()
     carried_back = jnp.zeros((WIDE, WIDE), F32)

time: 117 us -> 115 us (0.983)
  Pallas kernels: 111 us -> 109 us
    pallas_call x1, Pallas kernels: 111 us -> 109 us  [body(): pl.pallas_call(kernel, out_shape=shapes, in_specs=[spec] * 7, out_specs=(...]
where the time goes in v4:
time: 115 us
  Pallas kernels  109 us (95%)
  local copies, waits for them, and re-layouts  5.24 us (5%)
    pallas_call x1, Pallas kernels, body(): pl.pallas_call(kernel, out_shape=shapes, in_specs=[spec] * 7, out_specs=(...  109 us
    unnamed x10, local copies, waits for them, and re-layouts  5.24 us

profile of v4, /device:TPU:4, one launch (start us, length us, event | category | flops | bytes accessed | tf_op | source)
XLA Modules:
  0.0 115.0 jit_solution(16806662535501024058)
XLA Ops:
  0.6 109.1 %shard_map.102 = (bf16[512,1024]{1,0:T(8,128)(2,1)}, bf16[512,1024]{1,0:T(8,128)(2,1)}, bf16[512,1024]{1,0:T(8,128)(2,1)}, f32[192,1024]{1,0:T(8,128)}) custom-call(bf16[512,1024]{1,0:T(8,128)(2,1)} %q.1, bf16[512,1024]{1,0:T(8,128)(2,1)} %k.1, bf16[512,1024]{1,0:T(8,128)(2,1)} %v.1, f32[8,512]{1,0:T(8,128)} %ld.1, f32[1,1024]{1,0:T(1,128)} %bitcast.1, ...), custom_call_target="tpu_custom_call" | custom-call | tf_op jit(solution)/shard_map/pallas_call | solution.py:774
  109.8 0.0 copy-start.1
  109.8 0.0 copy-start
  109.8 2.4 %copy.15 = bf16[512,1024]{1,0:T(8,128)(2,1)} copy(bf16[512,1024]{1,0:T(8,128)(2,1)} %get-tuple-element.8) | data formatting | bytes 2097152
  112.2 0.0 copy-done.1
  112.2 0.0 copy-start.2
  112.2 1.0 copy.16
  113.2 0.0 copy-done
  113.2 1.0 copy.17
  114.1 0.0 copy-done.2
  114.1 0.9 copy.18
Async XLA Ops:
  109.8 2.4 %copy-start.1 = (bf16[512,1024]{1,0:T(8,128)(2,1)S(1)}, bf16[512,1024]{1,0:T(8,128)(2,1)}, u32[]{:S(2)}) copy-start(bf16[512,1024]{1,0:T(8,128)(2,1)} %get-tuple-element.9) | copy-start | bytes 3145732
  109.8 3.4 %copy-start = (bf16[512,1024]{1,0:T(8,128)(2,1)S(1)}, bf16[512,1024]{1,0:T(8,128)(2,1)}, u32[]{:S(2)}) copy-start(bf16[512,1024]{1,0:T(8,128)(2,1)} %get-tuple-element.10) | copy-start | bytes 3145732
  112.2 1.9 %copy-start.2 = (f32[192,1024]{1,0:T(8,128)S(1)}, f32[192,1024]{1,0:T(8,128)}, u32[]{:S(2)}) copy-start(f32[192,1024]{1,0:T(8,128)} %get-tuple-element.11) | copy-start | bytes 2359300
